TPU v7x, 512 devices: a whole 4x4x16 slice. The times are simulated.
512 devices in a mesh: wide: 64 (over z, y), narrow: 8 (over x, core).
Axes of the slice: x: 4, y: 4, z: 16, core: 2. Of those that a mesh axis runs over, the one named last changes fastest.
Arguments:
- density: bfloat16 [1024, 64, 2048], P('wide', 'narrow'), may hold values from 0 to 1
- color_table: bfloat16 [3, 256], replicated, may hold values from 0 to 1
- opacity_table: bfloat16 [256], replicated, may hold values from 9.760261e-07 to 0.01953125
- view_shear: int32 [1], replicated, may hold values from -512 to 512
Outputs:
- image: float32 [4, 64, 2048], P(None, 'narrow', 'wide')
All inputs are finite; a program needn't handle non-finite values.
Results may differ from a plain program's by a relative error of at most 0.0003.
Values may be sent and summed in bfloat16 or wider, within the bound.
No kernel may reach another device: no remote copies, remote signals or barrier semaphores. Data moves between devices by JAX's collectives and lax.ppermute only.
A program may use at most 64 MiB of HBM per device.

v0:
```python
import math

import jax
import jax.numpy as jnp
from jax import lax
from jax.sharding import PartitionSpec as P

light_across = 0.48
light_down = 0.6
light_depth = 0.64


def with_halo(block, sides, width):
    for axis, dim in sides:
        count = lax.axis_size(axis)
        forward = [(i, i + 1) for i in range(count - 1)]
        backward = [(target, source) for source, target in forward]
        low = lax.ppermute(
            lax.slice_in_dim(block, block.shape[dim] - width, None, axis=dim), axis, forward
        )
        high = lax.ppermute(lax.slice_in_dim(block, 0, width, axis=dim), axis, backward)
        block = jnp.concatenate([low, block, high], axis=dim)
    return block


def shade_slice(layers, lookup):
    middle = layers[1, 1:-1]
    widened = jnp.pad(middle, ((0, 0), (1, 1)))
    slope_across = 0.5 * (widened[:, 2:] - widened[:, :-2])
    slope_down = 0.5 * (layers[1, 2:] - layers[1, :-2])
    slope_depth = 0.5 * (layers[2, 1:-1] - layers[0, 1:-1])
    facing = light_across * slope_across + light_down * slope_down + light_depth * slope_depth
    strength = (
        slope_across * slope_across + slope_down * slope_down + slope_depth * slope_depth + 0.05
    )
    shading = 0.3 + 0.7 * facing * facing / strength
    scaled = middle * 255.0
    floor_level = jnp.clip(jnp.floor(scaled), 0.0, 254.0)
    fraction = scaled - floor_level
    low_values, high_values = lookup(floor_level)
    sampled = low_values + fraction * (high_values - low_values)
    opacity = sampled[3]
    premult = sampled[:3] * shading * opacity
    return jnp.concatenate([premult, opacity[None]], 0)


def resample(plane_values, slice_global, depth_total, shear_value):
    numerator = shear_value * (2 * slice_global + 1 - depth_total)
    denominator = 2 * depth_total
    whole_shift = jnp.floor_divide(numerator, denominator)
    offset = (numerator - whole_shift * denominator).astype(jnp.float32) / denominator
    column_count = plane_values.shape[2]
    margin = column_count // 2
    widened = jnp.pad(plane_values, ((0, 0), (0, 0), (margin, margin)))
    aligned = lax.dynamic_slice_in_dim(widened, margin - whole_shift, column_count, 2)
    earlier = lax.dynamic_slice_in_dim(widened, margin - whole_shift - 1, column_count, 2)
    return offset * earlier + (1.0 - offset) * aligned


def per_device(density, color_table, opacity_table, view_shear):
    depth_local, row_count, column_count = density.shape
    wide_count = lax.axis_size("wide")
    depth_total = depth_local * wide_count
    depth_start = lax.axis_index("wide") * depth_local
    shear_value = view_shear[0]
    flip_on = jnp.remainder(shear_value, 2)
    padded = with_halo(density, (("wide", 0), ("narrow", 1)), 1)
    lookup_table = jnp.concatenate([color_table, opacity_table[None]], 0)
    shifted_table = jnp.concatenate([lookup_table[:, 1:], lookup_table[:, -1:]], 1)
    stacked_table = jnp.concatenate([lookup_table, shifted_table], 0)
    level_count = stacked_table.shape[1]
    level_ids = jnp.arange(level_count, dtype=jnp.int32)

    def lookup(floor_level):
        level_index = floor_level.astype(jnp.int32)

        def one_row(row_levels):
            selector = (level_ids[:, None] == row_levels[None, :]).astype(jnp.bfloat16)
            return jnp.dot(stacked_table, selector, preferred_element_type=jnp.float32)

        looked_up = jnp.moveaxis(lax.map(one_row, level_index), 1, 0)
        return (looked_up[:4], looked_up[4:])

    def shade_one(layers, slice_global):
        return resample(shade_slice(layers, lookup), slice_global, depth_total, shear_value)

    block_size = math.gcd(depth_local, 8)

    def advance(carried, counter):
        block_start = jnp.where(
            flip_on == 1, depth_local - block_size * (counter + 1), counter * block_size
        )
        slab = lax.dynamic_slice_in_dim(padded, block_start, block_size + 2, 0).astype(jnp.float32)
        windows = jnp.stack([slab[within : within + 3] for within in range(block_size)], 0)
        slice_ids = depth_start + block_start + jnp.arange(block_size, dtype=jnp.int32)
        planes = jax.vmap(shade_one)(windows, slice_ids)
        for within in range(block_size):
            premult_sum, transmit = carried
            position = jnp.where(flip_on == 1, block_size - 1 - within, within).astype(jnp.int32)
            plane_values = lax.dynamic_index_in_dim(planes, position, 0, keepdims=False)
            carried = (
                premult_sum + transmit * plane_values[:3],
                transmit * (1.0 - plane_values[3]),
            )
        return (carried, None)

    starting = (
        jnp.zeros((3, row_count, column_count), jnp.float32),
        jnp.ones((row_count, column_count), jnp.float32),
    )
    finished, ignored = lax.scan(
        advance, starting, jnp.arange(depth_local // block_size, dtype=jnp.int32)
    )
    premult_sum, transmit = finished
    brick = jnp.concatenate([premult_sum, transmit[None]], 0)
    gathered = lax.all_to_all(brick[None], "wide", split_axis=3, concat_axis=0, tiled=True)
    transmit_all = gathered[:, 3]
    unity = jnp.ones_like(transmit_all[:1])
    forward = jnp.cumprod(transmit_all, axis=0)
    forward = jnp.concatenate([unity, forward[:-1]], 0)
    backward = jnp.cumprod(transmit_all[::-1], axis=0)[::-1]
    backward = jnp.concatenate([backward[1:], unity], 0)
    before = jnp.where(flip_on == 1, backward, forward)
    colour = jnp.sum(before[:, None] * gathered[:, :3], axis=0)
    through = jnp.prod(transmit_all, axis=0)
    return jnp.concatenate([colour, (1.0 - through)[None]], 0)


def solution(mesh):
    placed = (P("wide", "narrow", None), P(), P(), P())
    return jax.shard_map(
        per_device, mesh=mesh, in_specs=placed, out_specs=P(None, "narrow", "wide"), check_vma=False
    )
```

profile of v0, /device:TPU:2, one launch (start us, length us, event | category | flops | bytes accessed | tf_op | source)
XLA Modules:
  0.0 441.6 jit_solution(5385762717100863339)
XLA Ops:
  19.1 353.8 %while.59 = (s32[]{:T(128)}, f32[3,8,2048]{2,1,0:T(8,128)S(1)}, f32[8,2048]{1,0:T(8,128)S(1)}, s32[]{:T(128)}, s32[2]{0:T(128)S(1)}, /*index=5*/pred[]{:T(512)},...) while((s32[]{:T(128)}, f32[3,8,2048]{2,1,0:T(8,128)S(1)}, ...), condition=%wide.region_3.4_spmd.clone, body=%wide.region_0.3_spmd.clone.sunk | while | flops 86647264 | bytes 58564144 | solution.py:111
  22.1 111.9 %while.60 = (s32[]{:T(128)}, f32[8,8,8,2048]{3,0,2,1:T(8,128)}, s32[256]{0:T(256)S(1)}, s32[8,8,2048]{2,0,1:T(8,128)S(1)}, bf16[8,256]{1,0:T(8,128)(2,1)S(1)}, /*index=5*/s32[]{:T(128)}, s32[]{:T(128)}) while((s32[]{:T(128)}, f32[8,8,8,2048]{3,0,2,1:T(8,128)}, s32[256]{0:T(256)S(1)}, s32[8,8,2048]{2,0,1:T(8,128)S(1)}, ...), condition=%wide.region_2.2_spmd, body=%wide.region_1.1_spmd.sunk | while | flops 71303168 | bytes 2954325 | solution.py:81
  25.4 10.7 %dynamic_update_slice.5 = f32[8,8,8,2048]{3,0,2,1:T(8,128)} dynamic-update-slice(f32[8,8,8,2048]{3,0,2,1:T(8,128)} %get-tuple-element.863, f32[1,8,8,2048]{3,0,2,1:T(1,128)S(1)} %copy.96, s32[]{:T(128)} %get-tuple-element.862, s32[]{:T(128)} %constant.324.clone.1..sunk.1..sunk, s32[]{:T(128)} %constant.324.clone.1..sunk.1..sunk, s32[]{:T(128)} %constant.324.clone.1..sunk.1..sunk) | dynamic-update-slice | bytes 1048580 | tf_op jit(solution)/shard_map/while/body/eval_jaxpr/vmap()/while/body/jit(dynamic_update_index_in_dim)/dynamic_update_slice | solution.py:81
  39.3 10.7 %dynamic_update_slice.5 = f32[8,8,8,2048]{3,0,2,1:T(8,128)} dynamic-update-slice(f32[8,8,8,2048]{3,0,2,1:T(8,128)} %get-tuple-element.863, f32[1,8,8,2048]{3,0,2,1:T(1,128)S(1)} %copy.96, s32[]{:T(128)} %get-tuple-element.862, s32[]{:T(128)} %constant.324.clone.1..sunk.1..sunk, s32[]{:T(128)} %constant.324.clone.1..sunk.1..sunk, s32[]{:T(128)} %constant.324.clone.1..sunk.1..sunk) | dynamic-update-slice | bytes 1048580 | tf_op jit(solution)/shard_map/while/body/eval_jaxpr/vmap()/while/body/jit(dynamic_update_index_in_dim)/dynamic_update_slice | solution.py:81
  53.3 10.7 %dynamic_update_slice.5 = f32[8,8,8,2048]{3,0,2,1:T(8,128)} dynamic-update-slice(f32[8,8,8,2048]{3,0,2,1:T(8,128)} %get-tuple-element.863, f32[1,8,8,2048]{3,0,2,1:T(1,128)S(1)} %copy.96, s32[]{:T(128)} %get-tuple-element.862, s32[]{:T(128)} %constant.324.clone.1..sunk.1..sunk, s32[]{:T(128)} %constant.324.clone.1..sunk.1..sunk, s32[]{:T(128)} %constant.324.clone.1..sunk.1..sunk) | dynamic-update-slice | bytes 1048580 | tf_op jit(solution)/shard_map/while/body/eval_jaxpr/vmap()/while/body/jit(dynamic_update_index_in_dim)/dynamic_update_slice | solution.py:81
  67.3 10.7 %dynamic_update_slice.5 = f32[8,8,8,2048]{3,0,2,1:T(8,128)} dynamic-update-slice(f32[8,8,8,2048]{3,0,2,1:T(8,128)} %get-tuple-element.863, f32[1,8,8,2048]{3,0,2,1:T(1,128)S(1)} %copy.96, s32[]{:T(128)} %get-tuple-element.862, s32[]{:T(128)} %constant.324.clone.1..sunk.1..sunk, s32[]{:T(128)} %constant.324.clone.1..sunk.1..sunk, s32[]{:T(128)} %constant.324.clone.1..sunk.1..sunk) | dynamic-update-slice | bytes 1048580 | tf_op jit(solution)/shard_map/while/body/eval_jaxpr/vmap()/while/body/jit(dynamic_update_index_in_dim)/dynamic_update_slice | solution.py:81
  81.3 10.7 %dynamic_update_slice.5 = f32[8,8,8,2048]{3,0,2,1:T(8,128)} dynamic-update-slice(f32[8,8,8,2048]{3,0,2,1:T(8,128)} %get-tuple-element.863, f32[1,8,8,2048]{3,0,2,1:T(1,128)S(1)} %copy.96, s32[]{:T(128)} %get-tuple-element.862, s32[]{:T(128)} %constant.324.clone.1..sunk.1..sunk, s32[]{:T(128)} %constant.324.clone.1..sunk.1..sunk, s32[]{:T(128)} %constant.324.clone.1..sunk.1..sunk) | dynamic-update-slice | bytes 1048580 | tf_op jit(solution)/shard_map/while/body/eval_jaxpr/vmap()/while/body/jit(dynamic_update_index_in_dim)/dynamic_update_slice | solution.py:81
  95.3 10.7 %dynamic_update_slice.5 = f32[8,8,8,2048]{3,0,2,1:T(8,128)} dynamic-update-slice(f32[8,8,8,2048]{3,0,2,1:T(8,128)} %get-tuple-element.863, f32[1,8,8,2048]{3,0,2,1:T(1,128)S(1)} %copy.96, s32[]{:T(128)} %get-tuple-element.862, s32[]{:T(128)} %constant.324.clone.1..sunk.1..sunk, s32[]{:T(128)} %constant.324.clone.1..sunk.1..sunk, s32[]{:T(128)} %constant.324.clone.1..sunk.1..sunk) | dynamic-update-slice | bytes 1048580 | tf_op jit(solution)/shard_map/while/body/eval_jaxpr/vmap()/while/body/jit(dynamic_update_index_in_dim)/dynamic_update_slice | solution.py:81
  109.2 10.7 %dynamic_update_slice.5 = f32[8,8,8,2048]{3,0,2,1:T(8,128)} dynamic-update-slice(f32[8,8,8,2048]{3,0,2,1:T(8,128)} %get-tuple-element.863, f32[1,8,8,2048]{3,0,2,1:T(1,128)S(1)} %copy.96, s32[]{:T(128)} %get-tuple-element.862, s32[]{:T(128)} %constant.324.clone.1..sunk.1..sunk, s32[]{:T(128)} %constant.324.clone.1..sunk.1..sunk, s32[]{:T(128)} %constant.324.clone.1..sunk.1..sunk) | dynamic-update-slice | bytes 1048580 | tf_op jit(solution)/shard_map/while/body/eval_jaxpr/vmap()/while/body/jit(dynamic_update_index_in_dim)/dynamic_update_slice | solution.py:81
  123.2 10.7 %dynamic_update_slice.5 = f32[8,8,8,2048]{3,0,2,1:T(8,128)} dynamic-update-slice(f32[8,8,8,2048]{3,0,2,1:T(8,128)} %get-tuple-element.863, f32[1,8,8,2048]{3,0,2,1:T(1,128)S(1)} %copy.96, s32[]{:T(128)} %get-tuple-element.862, s32[]{:T(128)} %constant.324.clone.1..sunk.1..sunk, s32[]{:T(128)} %constant.324.clone.1..sunk.1..sunk, s32[]{:T(128)} %constant.324.clone.1..sunk.1..sunk) | dynamic-update-slice | bytes 1048580 | tf_op jit(solution)/shard_map/while/body/eval_jaxpr/vmap()/while/body/jit(dynamic_update_index_in_dim)/dynamic_update_slice | solution.py:81
  140.3 23.6 %while.62 = (s32[]{:T(128)}, f32[8,4,8,4096]{3,2,1,0:T(8,128)}, s32[8,4]{0,1:T(4,128)S(1)}, f32[8,4,8,2048]{3,2,1,0:T(8,128)S(1)}, s32[]{:T(128)}) while((s32[]{:T(128)}, f32[8,4,8,4096]{3,2,1,0:T(8,128)}, s32[8,4]{0,1:T(4,128)S(1)}, f32[8,4,8,2048]{3,2,1,0:T(8,128)S(1)}, s32[]{:T(128)}) %tuple.137), condition=%wide.while_cond, body=%wide.while_body.sunk | while | flops 2 | bytes 524413 | solution.py:56
  165.5 23.7 %while.61 = (s32[]{:T(128)}, f32[8,4,8,4096]{3,2,1,0:T(8,128)}, s32[8,4]{0,1:T(4,128)S(1)}, f32[8,4,8,2048]{3,2,1,0:T(8,128)S(1)}, s32[]{:T(128)}) while((s32[]{:T(128)}, f32[8,4,8,4096]{3,2,1,0:T(8,128)}, s32[8,4]{0,1:T(4,128)S(1)}, f32[8,4,8,2048]{3,2,1,0:T(8,128)S(1)}, s32[]{:T(128)}) %tuple.143), condition=%wide.while_cond.1, body=%wide.while_body.1.sunk | while | flops 2 | bytes 524413 | solution.py:55
  199.0 111.9 %while.60 = (s32[]{:T(128)}, f32[8,8,8,2048]{3,0,2,1:T(8,128)}, s32[256]{0:T(256)S(1)}, s32[8,8,2048]{2,0,1:T(8,128)S(1)}, bf16[8,256]{1,0:T(8,128)(2,1)S(1)}, /*index=5*/s32[]{:T(128)}, s32[]{:T(128)}) while((s32[]{:T(128)}, f32[8,8,8,2048]{3,0,2,1:T(8,128)}, s32[256]{0:T(256)S(1)}, s32[8,8,2048]{2,0,1:T(8,128)S(1)}, ...), condition=%wide.region_2.2_spmd, body=%wide.region_1.1_spmd.sunk | while | flops 71303168 | bytes 2954325 | solution.py:81
  202.3 10.7 %dynamic_update_slice.5 = f32[8,8,8,2048]{3,0,2,1:T(8,128)} dynamic-update-slice(f32[8,8,8,2048]{3,0,2,1:T(8,128)} %get-tuple-element.863, f32[1,8,8,2048]{3,0,2,1:T(1,128)S(1)} %copy.96, s32[]{:T(128)} %get-tuple-element.862, s32[]{:T(128)} %constant.324.clone.1..sunk.1..sunk, s32[]{:T(128)} %constant.324.clone.1..sunk.1..sunk, s32[]{:T(128)} %constant.324.clone.1..sunk.1..sunk) | dynamic-update-slice | bytes 1048580 | tf_op jit(solution)/shard_map/while/body/eval_jaxpr/vmap()/while/body/jit(dynamic_update_index_in_dim)/dynamic_update_slice | solution.py:81
  216.2 10.7 %dynamic_update_slice.5 = f32[8,8,8,2048]{3,0,2,1:T(8,128)} dynamic-update-slice(f32[8,8,8,2048]{3,0,2,1:T(8,128)} %get-tuple-element.863, f32[1,8,8,2048]{3,0,2,1:T(1,128)S(1)} %copy.96, s32[]{:T(128)} %get-tuple-element.862, s32[]{:T(128)} %constant.324.clone.1..sunk.1..sunk, s32[]{:T(128)} %constant.324.clone.1..sunk.1..sunk, s32[]{:T(128)} %constant.324.clone.1..sunk.1..sunk) | dynamic-update-slice | bytes 1048580 | tf_op jit(solution)/shard_map/while/body/eval_jaxpr/vmap()/while/body/jit(dynamic_update_index_in_dim)/dynamic_update_slice | solution.py:81
  230.2 10.7 %dynamic_update_slice.5 = f32[8,8,8,2048]{3,0,2,1:T(8,128)} dynamic-update-slice(f32[8,8,8,2048]{3,0,2,1:T(8,128)} %get-tuple-element.863, f32[1,8,8,2048]{3,0,2,1:T(1,128)S(1)} %copy.96, s32[]{:T(128)} %get-tuple-element.862, s32[]{:T(128)} %constant.324.clone.1..sunk.1..sunk, s32[]{:T(128)} %constant.324.clone.1..sunk.1..sunk, s32[]{:T(128)} %constant.324.clone.1..sunk.1..sunk) | dynamic-update-slice | bytes 1048580 | tf_op jit(solution)/shard_map/while/body/eval_jaxpr/vmap()/while/body/jit(dynamic_update_index_in_dim)/dynamic_update_slice | solution.py:81
  244.2 10.7 %dynamic_update_slice.5 = f32[8,8,8,2048]{3,0,2,1:T(8,128)} dynamic-update-slice(f32[8,8,8,2048]{3,0,2,1:T(8,128)} %get-tuple-element.863, f32[1,8,8,2048]{3,0,2,1:T(1,128)S(1)} %copy.96, s32[]{:T(128)} %get-tuple-element.862, s32[]{:T(128)} %constant.324.clone.1..sunk.1..sunk, s32[]{:T(128)} %constant.324.clone.1..sunk.1..sunk, s32[]{:T(128)} %constant.324.clone.1..sunk.1..sunk) | dynamic-update-slice | bytes 1048580 | tf_op jit(solution)/shard_map/while/body/eval_jaxpr/vmap()/while/body/jit(dynamic_update_index_in_dim)/dynamic_update_slice | solution.py:81
  258.2 10.7 %dynamic_update_slice.5 = f32[8,8,8,2048]{3,0,2,1:T(8,128)} dynamic-update-slice(f32[8,8,8,2048]{3,0,2,1:T(8,128)} %get-tuple-element.863, f32[1,8,8,2048]{3,0,2,1:T(1,128)S(1)} %copy.96, s32[]{:T(128)} %get-tuple-element.862, s32[]{:T(128)} %constant.324.clone.1..sunk.1..sunk, s32[]{:T(128)} %constant.324.clone.1..sunk.1..sunk, s32[]{:T(128)} %constant.324.clone.1..sunk.1..sunk) | dynamic-update-slice | bytes 1048580 | tf_op jit(solution)/shard_map/while/body/eval_jaxpr/vmap()/while/body/jit(dynamic_update_index_in_dim)/dynamic_update_slice | solution.py:81
  272.2 10.7 %dynamic_update_slice.5 = f32[8,8,8,2048]{3,0,2,1:T(8,128)} dynamic-update-slice(f32[8,8,8,2048]{3,0,2,1:T(8,128)} %get-tuple-element.863, f32[1,8,8,2048]{3,0,2,1:T(1,128)S(1)} %copy.96, s32[]{:T(128)} %get-tuple-element.862, s32[]{:T(128)} %constant.324.clone.1..sunk.1..sunk, s32[]{:T(128)} %constant.324.clone.1..sunk.1..sunk, s32[]{:T(128)} %constant.324.clone.1..sunk.1..sunk) | dynamic-update-slice | bytes 1048580 | tf_op jit(solution)/shard_map/while/body/eval_jaxpr/vmap()/while/body/jit(dynamic_update_index_in_dim)/dynamic_update_slice | solution.py:81
  286.1 10.7 %dynamic_update_slice.5 = f32[8,8,8,2048]{3,0,2,1:T(8,128)} dynamic-update-slice(f32[8,8,8,2048]{3,0,2,1:T(8,128)} %get-tuple-element.863, f32[1,8,8,2048]{3,0,2,1:T(1,128)S(1)} %copy.96, s32[]{:T(128)} %get-tuple-element.862, s32[]{:T(128)} %constant.324.clone.1..sunk.1..sunk, s32[]{:T(128)} %constant.324.clone.1..sunk.1..sunk, s32[]{:T(128)} %constant.324.clone.1..sunk.1..sunk) | dynamic-update-slice | bytes 1048580 | tf_op jit(solution)/shard_map/while/body/eval_jaxpr/vmap()/while/body/jit(dynamic_update_index_in_dim)/dynamic_update_slice | solution.py:81
  300.1 10.7 %dynamic_update_slice.5 = f32[8,8,8,2048]{3,0,2,1:T(8,128)} dynamic-update-slice(f32[8,8,8,2048]{3,0,2,1:T(8,128)} %get-tuple-element.863, f32[1,8,8,2048]{3,0,2,1:T(1,128)S(1)} %copy.96, s32[]{:T(128)} %get-tuple-element.862, s32[]{:T(128)} %constant.324.clone.1..sunk.1..sunk, s32[]{:T(128)} %constant.324.clone.1..sunk.1..sunk, s32[]{:T(128)} %constant.324.clone.1..sunk.1..sunk) | dynamic-update-slice | bytes 1048580 | tf_op jit(solution)/shard_map/while/body/eval_jaxpr/vmap()/while/body/jit(dynamic_update_index_in_dim)/dynamic_update_slice | solution.py:81
  317.2 23.6 %while.62 = (s32[]{:T(128)}, f32[8,4,8,4096]{3,2,1,0:T(8,128)}, s32[8,4]{0,1:T(4,128)S(1)}, f32[8,4,8,2048]{3,2,1,0:T(8,128)S(1)}, s32[]{:T(128)}) while((s32[]{:T(128)}, f32[8,4,8,4096]{3,2,1,0:T(8,128)}, s32[8,4]{0,1:T(4,128)S(1)}, f32[8,4,8,2048]{3,2,1,0:T(8,128)S(1)}, s32[]{:T(128)}) %tuple.137), condition=%wide.while_cond, body=%wide.while_body.sunk | while | flops 2 | bytes 524413 | solution.py:56
  342.4 23.7 %while.61 = (s32[]{:T(128)}, f32[8,4,8,4096]{3,2,1,0:T(8,128)}, s32[8,4]{0,1:T(4,128)S(1)}, f32[8,4,8,2048]{3,2,1,0:T(8,128)S(1)}, s32[]{:T(128)}) while((s32[]{:T(128)}, f32[8,4,8,4096]{3,2,1,0:T(8,128)}, s32[8,4]{0,1:T(4,128)S(1)}, f32[8,4,8,2048]{3,2,1,0:T(8,128)S(1)}, s32[]{:T(128)}) %tuple.143), condition=%wide.while_cond.1, body=%wide.while_body.1.sunk | while | flops 2 | bytes 524413 | solution.py:55
  386.0 42.7 %all_to_all.18 = f32[64,1,1024]{2,1,0:T(1,128)S(1)} all-to-all(f32[64,1,1024]{2,1,0:T(1,128)S(1)} %reshape.310), channel_id=1, replica_groups=mesh['wide'=64,'narrow'=8] {'wide'}, dimensions={0} | all-to-all | bytes 524288 | tf_op jit(solution)/shard_map/all_to_all | solution.py:116
  (258 shorter events, 222.5 us)
Async XLA Ops:
  0.8 6.9 %collective-permute-start = (bf16[1,8,2048]{2,1,0:T(8,128)(2,1)S(1)}, bf16[1,8,2048]{2,1,0:T(8,128)(2,1)S(1)}, u32[]{:S(2)}, u32[]{:S(2)}) collective-permute-start(bf16[1,8,2048]{2,1,0:T(8,128)(2,1)S(1)} %get-tuple-element.587), channel_id=1, source_target_pairs={{0,8},{8,16},{16,24},{24,32},{32,40},{40,48},{48,56},{56,64},{64,7... | collective-permute-start | bytes 98312 | tf_op jit(solution)/shard_map/ppermute | solution.py:18
  4.3 5.8 %collective-permute-start.1 = (bf16[1,8,2048]{2,1,0:T(8,128)(2,1)S(1)}, bf16[1,8,2048]{2,1,0:T(8,128)(2,1)S(1)}, u32[]{:S(2)}, u32[]{:S(2)}) collective-permute-start(bf16[1,8,2048]{2,1,0:T(8,128)(2,1)S(1)} %get-tuple-element.586), channel_id=1, source_target_pairs={{8,0},{16,8},{24,16},{32,24},{40,32},{48,40},{56,48},{64,56},{72,6... | collective-permute-start | bytes 98312 | tf_op jit(solution)/shard_map/ppermute | solution.py:21
  10.3 6.5 %collective-permute-start.2 = (bf16[18,1,2048]{2,1,0:T(2,128)(2,1)S(1)}, bf16[18,1,2048]{2,1,0:T(2,128)(2,1)S(1)}, u32[]{:S(2)}, u32[]{:S(2)}) collective-permute-start(bf16[18,1,2048]{2,1,0:T(2,128)(2,1)S(1)} %get-tuple-element.584), channel_id=1, source_target_pairs={{0,1},{1,2},{2,3},{3,4},{4,5},{5,6},{6,7},{8,9},{9,10},{10,11},{11... | collective-permute-start | bytes 221192 | tf_op jit(solution)/shard_map/ppermute | solution.py:18
  12.2 6.3 %collective-permute-start.3 = (bf16[18,1,2048]{2,1,0:T(2,128)(2,1)S(1)}, bf16[18,1,2048]{2,1,0:T(2,128)(2,1)S(1)}, u32[]{:S(2)}, u32[]{:S(2)}) collective-permute-start(bf16[18,1,2048]{2,1,0:T(2,128)(2,1)S(1)} %get-tuple-element.585), channel_id=1, source_target_pairs={{1,0},{2,1},{3,2},{4,3},{5,4},{6,5},{7,6},{9,8},{10,9},{11,10},{12... | collective-permute-start | bytes 221192 | tf_op jit(solution)/shard_map/ppermute | solution.py:21
  163.9 1.3 copy-start
  340.8 1.3 copy-start
where the time goes:
time: 449 us; the launch traced here: 442 us
  local copies, waits for them, and re-layouts  307 us (68%)
  blocking collectives  42.7 us (10%)
  matrix products  41.7 us (9%)
  other arithmetic  32.1 us (7%)
  starting transfers between devices  10.3 us (2%)
    dynamic_update_slice x32, local copies, waits for them, and re-layouts, lookup(): looked_up = jnp.moveaxis(lax.map(one_row, level_index), 1, 0)  180 us
    gather x96, local copies, waits for them, and re-layouts  93.8 us
    all_to_all x1, blocking collectives, per_device(): lax.all_to_all(brick[None], 'wide', split_axis=3, concat_axis=0, tiled=True)  42.7 us
    dot_general x16, matrix products, one_row(): return jnp.dot(stacked_table, selector, preferred_element_type=jnp.float32)  41.7 us
    unnamed x5, local copies, waits for them, and re-layouts  17.3 us
  transfers between devices with their start and end apart: 4, of which 3 were waited for; matrix products, arithmetic and copies ran while one was open for 1% of the time, Pallas kernels for 0%

commit v1 on v0

v1 whole, which is shorter than its diff:
```python
import functools

import jax
import jax.numpy as jnp
from jax import lax
from jax.experimental import pallas as pl
from jax.experimental.pallas import tpu as pltpu
from jax.sharding import Mesh, PartitionSpec as P

LANES = 128
LEFT = 3
RIGHT = 2
UNROLL = 4
OUTSIDE = -1.0 / 512
LIMIT = 12 * 1024 * 1024


def lane_ids():
    return lax.broadcasted_iota(jnp.int32, (8, LANES), 1)


def row_ids():
    return lax.broadcasted_iota(jnp.int32, (8, LANES), 0)


def pick(table, index):
    return jnp.take_along_axis(table, index, axis=1, mode="promise_in_bounds")


def tile(t):
    return pl.ds(t * LANES, LANES)


def shift_of(shear, z, depth_total):
    numerator = shear * (2 * z + 1 - depth_total)
    denominator = 2 * depth_total
    bits = denominator.bit_length() - 1
    whole = lax.shift_right_arithmetic(numerator, bits)
    rest = numerator - lax.shift_left(whole, bits)
    return whole, rest.astype(jnp.float32) * (1.0 / denominator)


def split_shift(whole):
    hop = lax.shift_right_arithmetic(whole, 7)
    return hop, whole & 127


def next_lane(left, here, lanes):
    return jnp.where(lanes == 0, pltpu.roll(left, 1, 1), pltpu.roll(here, 1, 1))


def lookup_kernel(shear_ref, dens_ref, color_ref, opacity_ref,
                  sample_ref, front_ref, back_ref, alpha_ref, across_ref, deep_ref, down_ref,
                  field_ref, value_ref, opaque_ref, ahead_ref, *, depth_total, place):
    depth, rows, columns = dens_ref.shape
    tiles = columns // LANES
    lanes = lane_ids()
    rows8 = row_ids()
    shear = shear_ref[0]
    start = place() * depth
    flip = (shear & 1) == 1
    zero = jnp.zeros((8, LANES), jnp.float32)
    outside = jnp.full((8, LANES), OUTSIDE, jnp.float32)

    def widen(z, carry):
        for t in range(LEFT):
            field_ref[z, :, tile(t)] = outside
        for t in range(RIGHT):
            field_ref[z, :, tile(LEFT + tiles + t)] = outside
        field_ref[z, :, pl.ds(LEFT * LANES, columns)] = dens_ref[z].astype(jnp.float32)
        return carry

    lax.fori_loop(0, depth, widen, 0)

    def align(i, carry):
        for j in range(UNROLL):
            z = i * UNROLL + j
            whole, g = shift_of(shear, start + z, depth_total)
            hop, r = split_shift(whole)
            base = pl.multiple_of((1 - hop) * LANES, LANES)
            keep = lanes >= r
            rolled = [pltpu.roll(field_ref[z, :, pl.ds(base + t * LANES, LANES)], r, 1) for t in range(tiles + 2)]
            for t in range(tiles + 1):
                value_ref[z, :, tile(t)] = jnp.where(keep, rolled[t + 1], rolled[t])
        return carry

    lax.fori_loop(0, depth // UNROLL, align, 0)

    evens, odds = [], []
    half = (2 * lanes) & 127
    low = lanes < 64
    for c in range(4):
        row = (color_ref[c:c + 1, :] if c < 3 else opacity_ref[...]).astype(jnp.float32)
        first = jnp.broadcast_to(row[:, :LANES], (8, LANES))
        second = jnp.broadcast_to(row[:, LANES:], (8, LANES))
        evens.append(jnp.where(low, pick(first, half), pick(second, half)))
        odds.append(jnp.where(low, pick(first, half + 1), pick(second, half + 1)))

    def sample(z, carry):
        for t in range(tiles + 1):
            value = value_ref[z, :, tile(t)]
            scaled = value * 255.0
            level = jnp.minimum(scaled.astype(jnp.int32), 254)
            even = lax.shift_right_logical(level + 1, 1)
            odd = lax.shift_right_logical(level, 1)
            weight = jnp.abs(scaled - (2 * even).astype(jnp.float32))
            mixed = []
            for c in range(4):
                e = pick(evens[c], even)
                mixed.append(e + weight * (pick(odds[c], odd) - e))
            opacity = jnp.where(value >= 0.0, mixed[3], 0.0)
            for c in range(3):
                sample_ref[c, z, :, tile(t)] = mixed[c] * opacity
            opaque_ref[z, :, tile(t)] = opacity
        return carry

    lax.fori_loop(0, depth, sample, 0)

    for t in range(tiles + 1):
        alpha_ref[:, tile(t)] = zero
        ahead_ref[:, tile(t)] = zero

    def advance(i, carry):
        for j in range(UNROLL):
            step = i * UNROLL + j
            z = jnp.where(flip, depth - 1 - step, step)
            whole, g = shift_of(shear, start + z, depth_total)
            opaque = [opaque_ref[z, :, tile(t)] for t in range(tiles + 1)]
            later = [pltpu.roll(v, 1, 1) for v in opaque]
            sooner = [pltpu.roll(v, LANES - 1, 1) for v in opaque] + [zero]
            for t in range(tiles + 1):
                right = jnp.where(lanes == LANES - 1, sooner[t + 1], sooner[t])
                ahead = ahead_ref[:, tile(t)]
                through = 1.0 - ahead
                front_ref[z, :, tile(t)] = g * through
                ahead_ref[:, tile(t)] = ahead + through * (right + g * (opaque[t] - right))
                if t:
                    left = jnp.where(lanes == 0, later[t - 1], later[t])
                    alpha = alpha_ref[:, tile(t)]
                    through = 1.0 - alpha
                    back_ref[z, :, tile(t)] = through - g * through
                    alpha_ref[:, tile(t)] = alpha + through * (opaque[t] + g * (left - opaque[t]))
                else:
                    back_ref[z, :, tile(t)] = zero
        return carry

    lax.fori_loop(0, depth // UNROLL, advance, 0)

    def slopes(i, carry):
        for j in range(UNROLL):
            z = i * UNROLL + j
            before = lax.max(z - 1, 0)
            after = lax.min(z + 1, depth - 1)
            inner_low = jnp.where(z > 0, 1.0, 0.0)
            inner_high = jnp.where(z < depth - 1, 1.0, 0.0)
            slabs = [field_ref[z, :, tile(LEFT + t)] for t in range(tiles)]
            later = [zero] + [pltpu.roll(v, 1, 1) for v in slabs]
            sooner = [pltpu.roll(v, LANES - 1, 1) for v in slabs] + [zero]
            for t in range(tiles):
                left = jnp.where(lanes == 0, later[t], later[t + 1])
                right = jnp.where(lanes == LANES - 1, sooner[t + 1], sooner[t])
                below = jnp.where(rows8 == 7, 0.0, pltpu.roll(slabs[t], 7, 0))
                above = jnp.where(rows8 == 0, 0.0, pltpu.roll(slabs[t], 1, 0))
                across_ref[z, :, tile(t)] = right - left
                down_ref[z, :, tile(t)] = below - above
                deep_ref[z, :, tile(t)] = (inner_high * field_ref[after, :, tile(LEFT + t)]
                                           - inner_low * field_ref[before, :, tile(LEFT + t)])
        return carry

    lax.fori_loop(0, depth // UNROLL, slopes, 0)


def shade_kernel(shear_ref, sample_ref, front_ref, back_ref, alpha_ref, across_ref, deep_ref, down_ref,
                 lo_ref, hi_ref, dn_ref, up_ref,
                 out_ref, shade_ref, moved_ref, above_ref, below_ref, now_ref, late_ref, *, depth_total, place):
    depth, rows, columns = across_ref.shape
    tiles = columns // LANES
    lanes = lane_ids()
    rows8 = row_ids()
    shear = shear_ref[0]
    start = place() * depth
    zero = jnp.zeros((8, LANES), jnp.float32)

    above_ref[...] = -dn_ref[...].astype(jnp.float32)
    below_ref[...] = up_ref[...].astype(jnp.float32)
    for z in range(depth):
        for t in range(LEFT):
            shade_ref[z, :, tile(t)] = zero
        for t in range(RIGHT):
            shade_ref[z, :, tile(LEFT + tiles + t)] = zero

    def shade(t, carry):
        here = pl.ds(pl.multiple_of(t * LANES, LANES), LANES)
        there = pl.ds(pl.multiple_of((t + LEFT) * LANES, LANES), LANES)
        for z in range(depth):
            above = jnp.broadcast_to(above_ref[z:z + 1, here], (8, LANES))
            below = jnp.broadcast_to(below_ref[z:z + 1, here], (8, LANES))
            extra = jnp.where(rows8 == 0, above, jnp.where(rows8 == 7, below, 0.0))
            down = down_ref[z, :, here] + extra
            deep = deep_ref[z, :, here]
            if z == 0:
                deep = deep - lo_ref[:, here].astype(jnp.float32)
            if z == depth - 1:
                deep = deep + hi_ref[:, here].astype(jnp.float32)
            across = across_ref[z, :, here]
            facing = 0.48 * across + 0.6 * down + 0.64 * deep
            strength = across * across + down * down + (deep * deep + 0.2)
            shade_ref[z, :, there] = 0.3 + 0.7 * facing * facing / strength
        return carry

    lax.fori_loop(0, tiles, shade, 0)

    def align(i, carry):
        for j in range(UNROLL):
            z = i * UNROLL + j
            whole, g = shift_of(shear, start + z, depth_total)
            hop, r = split_shift(whole)
            base = pl.multiple_of((1 - hop) * LANES, LANES)
            keep = lanes >= r
            rolled = [pltpu.roll(shade_ref[z, :, pl.ds(base + t * LANES, LANES)], r, 1) for t in range(tiles + 2)]
            for t in range(tiles + 1):
                moved_ref[z, :, tile(t)] = jnp.where(keep, rolled[t + 1], rolled[t])
        return carry

    lax.fori_loop(0, depth // UNROLL, align, 0)

    def gather(t, carry):
        here = pl.ds(pl.multiple_of(t * LANES, LANES), LANES)
        late = [zero] * 3
        now = [zero] * 3
        for z in range(depth):
            shading = moved_ref[z, :, here]
            front = front_ref[z, :, here] * shading
            back = back_ref[z, :, here] * shading
            for c in range(3):
                value = sample_ref[c, z, :, here]
                late[c] = late[c] + front * value
                now[c] = now[c] + back * value
        for c in range(3):
            late_ref[c, :, here] = late[c]
            now_ref[c, :, here] = now[c]
        return carry

    lax.fori_loop(0, tiles + 1, gather, 0)

    quarter = lax.shift_right_logical(lanes, 5)
    late = [[pltpu.roll(late_ref[c, :, tile(t)], 1, 1) for t in range(tiles + 1)] for c in range(3)]
    for t in range(tiles):
        parts = [now_ref[c, :, tile(t + 1)] + jnp.where(lanes == 0, late[c][t], late[c][t + 1]) for c in range(3)]
        parts.append(alpha_ref[:, tile(t + 1)])
        for y in range(4):
            moved = [parts[c] if c == y else pltpu.roll(parts[c], (32 * (c - y)) % LANES, 1) for c in range(4)]
            out_ref[4 * t + y] = jnp.where(quarter < 2, jnp.where(quarter == 0, moved[0], moved[1]),
                                           jnp.where(quarter == 2, moved[2], moved[3]))


def merge_kernel(shear_ref, parts_ref, out_ref):
    count = parts_ref.shape[0]
    lanes = lane_ids()
    flip = (shear_ref[0] & 1) == 1
    owner = 96 + (lanes & 31)
    total = jnp.zeros((8, LANES), jnp.float32)
    through = jnp.ones((8, LANES), jnp.float32)
    for i in range(count):
        block = parts_ref[jnp.where(flip, count - 1 - i, i)]
        total = total + through * block
        through = through - through * pick(block, owner)
    for c in range(4):
        out_ref[c] = total[:, 32 * c:32 * c + 32]


def per_device(density, color_table, opacity_table, view_shear, place=None, halos=None):
    depth, rows, columns = density.shape
    wide = 64
    depth_total = depth * wide
    if place is None:
        place = lambda: lax.axis_index("wide")
    f32 = jnp.float32
    vmem = pl.BlockSpec(memory_space=pltpu.VMEM)
    smem = pl.BlockSpec(memory_space=pltpu.SMEM)
    if halos is None:
        up_wide = [(i, i + 1) for i in range(wide - 1)]
        down_wide = [(b, a) for a, b in up_wide]
        up_narrow = [(i, i + 1) for i in range(7)]
        down_narrow = [(b, a) for a, b in up_narrow]
        lo = lax.ppermute(density[-1], "wide", up_wide)
        hi = lax.ppermute(density[0], "wide", down_wide)
        dn = lax.ppermute(density[:, -1], "narrow", up_narrow)
        up = lax.ppermute(density[:, 0], "narrow", down_narrow)
    else:
        lo, hi, dn, up = halos
    slab = (depth, rows, columns)
    wider = (depth, rows, columns + LANES)
    widest = (depth, rows, columns + (LEFT + RIGHT) * LANES)
    row = (rows, columns + LANES)
    local = pl.pallas_call(
        functools.partial(lookup_kernel, depth_total=depth_total, place=place),
        in_specs=[smem, vmem, vmem, vmem],
        out_specs=[vmem] * 7,
        out_shape=[pltpu.VMEM((3,) + wider, f32), pltpu.VMEM(wider, f32), pltpu.VMEM(wider, f32), pltpu.VMEM(row, f32),
                   pltpu.VMEM(slab, f32), pltpu.VMEM(slab, f32), pltpu.VMEM(slab, f32)],
        scratch_shapes=[pltpu.VMEM(widest, f32), pltpu.VMEM(wider, f32), pltpu.VMEM(wider, f32), pltpu.VMEM(row, f32)],
        compiler_params=pltpu.CompilerParams(vmem_limit_bytes=LIMIT),
        cost_estimate=pl.CostEstimate(flops=30_000_000, bytes_accessed=10_000_000, transcendentals=0),
        name="lookup",
    )(view_shear, density, color_table, opacity_table[None])
    bricks = pl.pallas_call(
        functools.partial(shade_kernel, depth_total=depth_total, place=place),
        in_specs=[smem] + [vmem] * 11,
        out_specs=vmem,
        out_shape=jax.ShapeDtypeStruct((wide, rows, LANES), f32),
        scratch_shapes=[pltpu.VMEM(widest, f32), pltpu.VMEM(wider, f32), pltpu.VMEM((depth, columns), f32),
                        pltpu.VMEM((depth, columns), f32), pltpu.VMEM((3,) + row, f32), pltpu.VMEM((3,) + row, f32)],
        compiler_params=pltpu.CompilerParams(vmem_limit_bytes=LIMIT),
        name="shade",
    )(view_shear, *local, lo, hi, dn, up)
    if halos is not None:
        return bricks
    parts = lax.all_to_all(bricks, "wide", split_axis=0, concat_axis=0, tiled=True)
    return pl.pallas_call(
        merge_kernel,
        in_specs=[smem, vmem],
        out_specs=vmem,
        out_shape=jax.ShapeDtypeStruct((4, rows, 32), f32),
        name="merge",
    )(view_shear, parts)


def solution(mesh):
    placed = (P("wide", "narrow", None), P(), P(), P())
    return jax.shard_map(
        per_device, mesh=mesh, in_specs=placed, out_specs=P(None, "narrow", "wide"), check_vma=False
    )
```

time: 449 us -> 72.5 us (0.16); the launches traced: 442 us -> 72.1 us
  local copies, waits for them, and re-layouts: 307 us -> 3.68 us
  matrix products: 41.7 us -> 0 us
  other arithmetic: 32.1 us -> 0 us
  Pallas kernels: 0 us -> 13.5 us
    dynamic_update_slice x32 -> x0, local copies, waits for them, and re-layouts: 180 us -> none  [lookup(): looked_up = jnp.moveaxis(lax.map(one_row, level_index), 1, 0)]
    gather x96 -> x0, local copies, waits for them, and re-layouts: 93.8 us -> none
    dot_general x16 -> x0, matrix products: 41.7 us -> none  [one_row(): return jnp.dot(stacked_table, selector, preferred_element_type=jnp.float32)]
    add x8 -> x0, other arithmetic: 16.8 us -> none  [the longest x2 6.78 us: resample(): return offset * earlier + (1.0 - offset) * aligned]
    unnamed x5 -> x6, local copies, waits for them, and re-layouts: 17.3 us -> 0.77 us
    pallas_call x0 -> x3, Pallas kernels: none -> 13.5 us  [the longest x1 8.92 us: per_device(): pl.pallas_call(functools.partial(lookup_kernel, depth_total=depth_total,...]
    concatenate x7 -> x0, other arithmetic: 7.61 us -> none  [the longest x2 4.87 us: shade_slice(): return jnp.concatenate([premult, opacity[None]], 0)]
  transfers between devices with their start and end apart: 4 -> 4, of which waited for: 3 -> 0; matrix products, arithmetic and copies ran while one was open for 1% -> 2% of each run, Pallas kernels for 0% -> 12%
where the time goes in v1:
time: 72.5 us; the launch traced here: 72.1 us
  blocking collectives  42.7 us (59%)
  Pallas kernels  13.5 us (19%)
  starting transfers between devices  11.4 us (16%)
  local copies, waits for them, and re-layouts  3.68 us (5%)
  between operations  0.75 us (1%)
    all_to_all x1, blocking collectives, per_device(): lax.all_to_all(bricks, 'wide', split_axis=0, concat_axis=0, tiled=True)  42.7 us
    pallas_call x1, Pallas kernels, per_device(): pl.pallas_call(functools.partial(lookup_kernel, depth_total=depth_total,...  8.92 us
    ppermute x1, starting transfers between devices, per_device(): lo = lax.ppermute(density[-1], 'wide', up_wide)  4.55 us
    ppermute x1, starting transfers between devices, per_device(): up = lax.ppermute(density[:, 0], 'narrow', down_narrow)  3.64 us
    pallas_call x1, Pallas kernels, per_device(): pl.pallas_call(functools.partial(shade_kernel, depth_total=depth_total, p...  2.77 us
    ppermute x1, starting transfers between devices, per_device(): dn = lax.ppermute(density[:, -1], 'narrow', up_narrow)  1.92 us
    pallas_call x1, Pallas kernels, per_device(): pl.pallas_call(merge_kernel, in_specs=[smem, vmem], out_specs=vmem, out_s...  1.83 us
    slice x1, local copies, waits for them, and re-layouts, per_device(): up = lax.ppermute(density[:, 0], 'narrow', down_narrow)  1.46 us
  transfers between devices with their start and end apart: 4, of which 0 were waited for; matrix products, arithmetic and copies ran while one was open for 2% of the time, Pallas kernels for 12%

profile of v1, /device:TPU:2, one launch (start us, length us, event | category | flops | bytes accessed | tf_op | source)
XLA Modules:
  0.0 72.1 jit_solution(11638093129831604749)
XLA Ops:
  0.0 0.0 copy-start
  0.0 1.5 %fusion = (bf16[16,1,2048]{2,1,0:T(2,128)(2,1)S(1)}, bf16[16,1,2048]{2,1,0:T(2,128)(2,1)S(1)}) fusion(bf16[16,8,2048]{2,1,0:T(8,128)(2,1)} %dens_ref.1), kind=kLoop, calls=%fused_computation.4 | loop fusion | bytes 262144 | tf_op jit(solution)/shard_map/slice | solution.py:289
  1.5 1.9 %collective-permute-start.2 = (bf16[16,2048]{1,0:T(8,128)(2,1)S(1)}, bf16[16,2048]{1,0:T(8,128)(2,1)S(1)}, u32[]{:S(2)}, u32[]{:S(2)}) collective-permute-start(bf16[16,2048]{1,0:T(8,128)(2,1)S(1)} %bitcast.10), channel_id=1, source_target_pairs={{0,1},{1,2},{2,3},{3,4},{4,5},{5,6},{6,7},{8,9},{9,10},{10,11},{11... | collective-permute-start | bytes 196616 | tf_op jit(solution)/shard_map/ppermute | solution.py:288
  3.5 3.6 %collective-permute-start.3 = (bf16[16,2048]{1,0:T(8,128)(2,1)S(1)}, bf16[16,2048]{1,0:T(8,128)(2,1)S(1)}, u32[]{:S(2)}, u32[]{:S(2)}) collective-permute-start(bf16[16,2048]{1,0:T(8,128)(2,1)S(1)} %bitcast.11), channel_id=1, source_target_pairs={{1,0},{2,1},{3,2},{4,3},{5,4},{6,5},{7,6},{9,8},{10,9},{11,10},{12... | collective-permute-start | bytes 196616 | tf_op jit(solution)/shard_map/ppermute | solution.py:289
  7.1 0.8 %slice_bitcast_fusion = (bf16[8,2048]{1,0:T(8,128)(2,1)S(1)}, bf16[8,2048]{1,0:T(8,128)(2,1)S(1)}) fusion(bf16[16,8,2048]{2,1,0:T(8,128)(2,1)} %dens_ref.1), kind=kLoop, calls=%fused_computation.2 | loop fusion | bytes 131072 | tf_op jit(solution)/shard_map/squeeze | solution.py:287
  7.9 1.3 %collective-permute-start.1 = (bf16[8,2048]{1,0:T(8,128)(2,1)S(1)}, bf16[8,2048]{1,0:T(8,128)(2,1)S(1)}, u32[]{:S(2)}, u32[]{:S(2)}) collective-permute-start(bf16[8,2048]{1,0:T(8,128)(2,1)S(1)} %get-tuple-element.21), channel_id=1, source_target_pairs={{8,0},{16,8},{24,16},{32,24},{40,32},{48,40},{56,48},{64,56},{72,6... | collective-permute-start | bytes 98312 | tf_op jit(solution)/shard_map/ppermute | solution.py:287
  9.2 4.5 %collective-permute-start = (bf16[8,2048]{1,0:T(8,128)(2,1)S(1)}, bf16[8,2048]{1,0:T(8,128)(2,1)S(1)}, u32[]{:S(2)}, u32[]{:S(2)}) collective-permute-start(bf16[8,2048]{1,0:T(8,128)(2,1)S(1)} %get-tuple-element.22), channel_id=1, source_target_pairs={{0,8},{8,16},{16,24},{24,32},{32,40},{40,48},{48,56},{56,64},{64,7... | collective-permute-start | bytes 98312 | tf_op jit(solution)/shard_map/ppermute | solution.py:286
  14.4 0.7 broadcast_in_dim.3.opacity_ref
  15.1 0.0 copy-done
  15.1 0.0 copy-start.1
  15.1 0.7 copy-done.1
  15.8 8.9 %lookup.1 = (f32[3,16,8,2176]{3,2,1,0:T(8,128)S(1)}, f32[16,8,2176]{2,1,0:T(8,128)S(1)}, f32[16,8,2176]{2,1,0:T(8,128)S(1)}, f32[8,2176]{1,0:T(8,128)S(1)}, f32[...) custom-call(s32[1]{0:T(128)S(6)} %copy.13.shear_ref, ...), custom_call_target="tpu_custom_call" | custom-call | flops 30000000 | bytes 10000000 | tf_op jit(solution)/shard_map/lookup/pallas_call | solution.py:296
  24.7 0.0 collective-permute-done.1.hi_ref
  24.7 0.0 collective-permute-done.lo_ref
  24.7 0.0 collective-permute-done.2.dn_ref
  24.7 0.0 collective-permute-done.3.up_ref
  24.7 2.8 %shade.1 = f32[64,8,128]{2,1,0:T(8,128)S(1)} custom-call(s32[1]{0:T(128)S(6)} %copy.13.shear_ref, f32[3,16,8,2176]{3,2,1,0:T(8,128)S(1)} %get-tuple-element.12.sample_ref, f32[16,8,2176]{2,1,0:T(8,128)S(1)} %get-tuple-element.13.front_ref, f32[16,8,2176]{2,1,0:T(8,128)S(1)} %get-tuple-element.14.back_ref, f32[8,2176]{1,0:T(8,128)S(1)} %get-tuple-element.15.alpha_ref, ...), custom_call_target="tpu_custom_call" | custom-call | tf_op jit(solution)/shard_map/shade/pallas_call | solution.py:307
  27.5 42.7 %all_to_all.5.parts_ref = f32[64,8,128]{2,1,0:T(8,128)} all-to-all(f32[64,8,128]{2,1,0:T(8,128)S(1)} %shade.1), channel_id=1, replica_groups=mesh['wide'=64,'narrow'=8] {'wide'}, dimensions={0} | all-to-all | bytes 524288 | tf_op jit(solution)/shard_map/all_to_all | solution.py:319
  70.3 1.8 %merge.1 = f32[4,8,32]{2,1,0:T(8,128)} custom-call(s32[1]{0:T(128)S(6)} %copy.13.shear_ref, f32[64,8,128]{2,1,0:T(8,128)} %all_to_all.5.parts_ref), custom_call_target="tpu_custom_call" | custom-call | tf_op jit(solution)/shard_map/merge/pallas_call | solution.py:320
  (2 shorter events, 0.1 us)
Async XLA Ops:
  0.0 15.1 %copy-start = (bf16[16,8,2048]{2,1,0:T(8,128)(2,1)S(1)}, bf16[16,8,2048]{2,1,0:T(8,128)(2,1)}, u32[]{:S(2)}) copy-start(bf16[16,8,2048]{2,1,0:T(8,128)(2,1)} %dens_ref.1) | copy-start | bytes 1572868
  1.5 23.2 %collective-permute-start.2 = (bf16[16,2048]{1,0:T(8,128)(2,1)S(1)}, bf16[16,2048]{1,0:T(8,128)(2,1)S(1)}, u32[]{:S(2)}, u32[]{:S(2)}) collective-permute-start(bf16[16,2048]{1,0:T(8,128)(2,1)S(1)} %bitcast.10), channel_id=1, source_target_pairs={{0,1},{1,2},{2,3},{3,4},{4,5},{5,6},{6,7},{8,9},{9,10},{10,11},{11... | collective-permute-start | bytes 196616 | tf_op jit(solution)/shard_map/ppermute | solution.py:288
  3.5 21.2 %collective-permute-start.3 = (bf16[16,2048]{1,0:T(8,128)(2,1)S(1)}, bf16[16,2048]{1,0:T(8,128)(2,1)S(1)}, u32[]{:S(2)}, u32[]{:S(2)}) collective-permute-start(bf16[16,2048]{1,0:T(8,128)(2,1)S(1)} %bitcast.11), channel_id=1, source_target_pairs={{1,0},{2,1},{3,2},{4,3},{5,4},{6,5},{7,6},{9,8},{10,9},{11,10},{12... | collective-permute-start | bytes 196616 | tf_op jit(solution)/shard_map/ppermute | solution.py:289
  7.9 16.8 %collective-permute-start.1 = (bf16[8,2048]{1,0:T(8,128)(2,1)S(1)}, bf16[8,2048]{1,0:T(8,128)(2,1)S(1)}, u32[]{:S(2)}, u32[]{:S(2)}) collective-permute-start(bf16[8,2048]{1,0:T(8,128)(2,1)S(1)} %get-tuple-element.21), channel_id=1, source_target_pairs={{8,0},{16,8},{24,16},{32,24},{40,32},{48,40},{56,48},{64,56},{72,6... | collective-permute-start | bytes 98312 | tf_op jit(solution)/shard_map/ppermute | solution.py:287
  9.2 15.5 %collective-permute-start = (bf16[8,2048]{1,0:T(8,128)(2,1)S(1)}, bf16[8,2048]{1,0:T(8,128)(2,1)S(1)}, u32[]{:S(2)}, u32[]{:S(2)}) collective-permute-start(bf16[8,2048]{1,0:T(8,128)(2,1)S(1)} %get-tuple-element.22), channel_id=1, source_target_pairs={{0,8},{8,16},{16,24},{24,32},{32,40},{40,48},{48,56},{56,64},{64,7... | collective-permute-start | bytes 98312 | tf_op jit(solution)/shard_map/ppermute | solution.py:286
  15.1 0.7 copy-start.1

commit v2 on v1

--- a/solution.py
+++ b/solution.py
@@ -11,7 +11,12 @@
 LEFT = 3
 RIGHT = 2
 UNROLL = 4
+FEW = 4
 OUTSIDE = -1.0 / 512
+RATIO_STEPS = 65000.0
+LOG_SPAN = 26.0
+LOG_STEPS = 65534.0 / (LOG_SPAN - 1.85)
+TINY = 1e-12
 LIMIT = 12 * 1024 * 1024
 
 
@@ -47,6 +52,26 @@
 
 def next_lane(left, here, lanes):
     return jnp.where(lanes == 0, pltpu.roll(left, 1, 1), pltpu.roll(here, 1, 1))
+
+
+def phase(place):
+    return ((place * 39) & 63) * (1.0 / 64.0) if isinstance(place, int) else ((place * 39) & 63).astype(jnp.float32) * (1.0 / 64.0)
+
+
+def encode(colors, alpha, offset):
+    inverse = RATIO_STEPS / jnp.maximum(alpha, TINY)
+    parts = [jnp.minimum(c * inverse + 0.5, 65535.0) for c in colors]
+    level = jnp.log2(jnp.maximum(alpha, TINY)) * LOG_STEPS + (LOG_SPAN * LOG_STEPS + offset)
+    parts.append(jnp.clip(level, 0.0, 65535.0))
+    return [p.astype(jnp.int32) - 32768 for p in parts]
+
+
+def decode(codes, lanes, owner, offset):
+    value = codes.astype(jnp.int32).astype(jnp.float32) + 32768.0
+    level = pick(value, owner)
+    alpha = jnp.exp2((level + (0.5 - offset)) * (1.0 / LOG_STEPS) - LOG_SPAN)
+    alpha = jnp.where(level > 0.0, alpha, 0.0)
+    return alpha, alpha * jnp.where(lanes < 96, value * (1.0 / RATIO_STEPS), 1.0)
 
 
 def lookup_kernel(shear_ref, dens_ref, color_ref, opacity_ref,
@@ -90,31 +115,30 @@
     half = (2 * lanes) & 127
     low = lanes < 64
     for c in range(4):
-        row = (color_ref[c:c + 1, :] if c < 3 else opacity_ref[...]).astype(jnp.float32)
+        row = (color_ref[c:c + 1, :] if c < 3 else opacity_ref[...].reshape(1, -1)).astype(jnp.float32)
         first = jnp.broadcast_to(row[:, :LANES], (8, LANES))
         second = jnp.broadcast_to(row[:, LANES:], (8, LANES))
         evens.append(jnp.where(low, pick(first, half), pick(second, half)))
         odds.append(jnp.where(low, pick(first, half + 1), pick(second, half + 1)))
 
-    def sample(z, carry):
-        for t in range(tiles + 1):
+    def sample(i, carry):
+        for z, t in [(i * FEW + j, t) for j in range(FEW) for t in range(tiles + 1)]:
             value = value_ref[z, :, tile(t)]
             scaled = value * 255.0
             level = jnp.minimum(scaled.astype(jnp.int32), 254)
             even = lax.shift_right_logical(level + 1, 1)
             odd = lax.shift_right_logical(level, 1)
             weight = jnp.abs(scaled - (2 * even).astype(jnp.float32))
-            mixed = []
-            for c in range(4):
-                e = pick(evens[c], even)
-                mixed.append(e + weight * (pick(odds[c], odd) - e))
+            lower = [pick(table, even) for table in evens]
+            upper = [pick(table, odd) for table in odds]
+            mixed = [e + weight * (o - e) for e, o in zip(lower, upper)]
             opacity = jnp.where(value >= 0.0, mixed[3], 0.0)
             for c in range(3):
                 sample_ref[c, z, :, tile(t)] = mixed[c] * opacity
             opaque_ref[z, :, tile(t)] = opacity
         return carry
 
-    lax.fori_loop(0, depth, sample, 0)
+    lax.fori_loop(0, depth // FEW, sample, 0)
 
     for t in range(tiles + 1):
         alpha_ref[:, tile(t)] = zero
@@ -171,8 +195,8 @@
 
 
 def shade_kernel(shear_ref, sample_ref, front_ref, back_ref, alpha_ref, across_ref, deep_ref, down_ref,
-                 lo_ref, hi_ref, dn_ref, up_ref,
-                 out_ref, shade_ref, moved_ref, above_ref, below_ref, now_ref, late_ref, *, depth_total, place):
+                 slice_a_ref, slice_b_ref, row_a_ref, row_b_ref,
+                 out_ref, shade_ref, moved_ref, above_ref, below_ref, now_ref, late_ref, *, depth_total, place, across):
     depth, rows, columns = across_ref.shape
     tiles = columns // LANES
     lanes = lane_ids()
@@ -181,8 +205,12 @@
     start = place() * depth
     zero = jnp.zeros((8, LANES), jnp.float32)
 
-    above_ref[...] = -dn_ref[...].astype(jnp.float32)
-    below_ref[...] = up_ref[...].astype(jnp.float32)
+    wide_odd = (place() & 1) == 1
+    narrow_odd = (across() & 1) == 1
+    row_a = row_a_ref[...].astype(jnp.float32)
+    row_b = row_b_ref[...].astype(jnp.float32)
+    above_ref[...] = -jnp.where(narrow_odd, row_a, row_b)
+    below_ref[...] = jnp.where(narrow_odd, row_b, row_a)
     for z in range(depth):
         for t in range(LEFT):
             shade_ref[z, :, tile(t)] = zero
@@ -198,13 +226,16 @@
             extra = jnp.where(rows8 == 0, above, jnp.where(rows8 == 7, below, 0.0))
             down = down_ref[z, :, here] + extra
             deep = deep_ref[z, :, here]
-            if z == 0:
-                deep = deep - lo_ref[:, here].astype(jnp.float32)
-            if z == depth - 1:
-                deep = deep + hi_ref[:, here].astype(jnp.float32)
-            across = across_ref[z, :, here]
-            facing = 0.48 * across + 0.6 * down + 0.64 * deep
-            strength = across * across + down * down + (deep * deep + 0.2)
+            if z == 0 or z == depth - 1:
+                slice_a = slice_a_ref[:, here].astype(jnp.float32)
+                slice_b = slice_b_ref[:, here].astype(jnp.float32)
+                if z == 0:
+                    deep = deep - jnp.where(wide_odd, slice_a, slice_b)
+                else:
+                    deep = deep + jnp.where(wide_odd, slice_b, slice_a)
+            side = across_ref[z, :, here]
+            facing = 0.48 * side + 0.6 * down + 0.64 * deep
+            strength = side * side + down * down + (deep * deep + 0.2)
             shade_ref[z, :, there] = 0.3 + 0.7 * facing * facing / strength
         return carry
 
@@ -247,11 +278,12 @@
     late = [[pltpu.roll(late_ref[c, :, tile(t)], 1, 1) for t in range(tiles + 1)] for c in range(3)]
     for t in range(tiles):
         parts = [now_ref[c, :, tile(t + 1)] + jnp.where(lanes == 0, late[c][t], late[c][t + 1]) for c in range(3)]
-        parts.append(alpha_ref[:, tile(t + 1)])
+        parts = encode(parts, alpha_ref[:, tile(t + 1)], phase(place()))
         for y in range(4):
             moved = [parts[c] if c == y else pltpu.roll(parts[c], (32 * (c - y)) % LANES, 1) for c in range(4)]
-            out_ref[4 * t + y] = jnp.where(quarter < 2, jnp.where(quarter == 0, moved[0], moved[1]),
-                                           jnp.where(quarter == 2, moved[2], moved[3]))
+            block = jnp.where(quarter < 2, jnp.where(quarter == 0, moved[0], moved[1]),
+                              jnp.where(quarter == 2, moved[2], moved[3]))
+            out_ref[4 * t + y] = block.astype(jnp.int16)
 
 
 def merge_kernel(shear_ref, parts_ref, out_ref):
@@ -262,33 +294,39 @@
     total = jnp.zeros((8, LANES), jnp.float32)
     through = jnp.ones((8, LANES), jnp.float32)
     for i in range(count):
-        block = parts_ref[jnp.where(flip, count - 1 - i, i)]
-        total = total + through * block
-        through = through - through * pick(block, owner)
+        slot = jnp.where(flip, count - 1 - i, i)
+        alpha, value = decode(parts_ref[slot], lanes, owner, phase(slot))
+        total = total + through * value
+        through = through - through * alpha
     for c in range(4):
         out_ref[c] = total[:, 32 * c:32 * c + 32]
 
 
-def per_device(density, color_table, opacity_table, view_shear, place=None, halos=None):
+def pairs(count, start):
+    return [p for i in range(start, count - 1, 2) for p in ((i, i + 1), (i + 1, i))]
+
+
+def per_device(density, color_table, opacity_table, view_shear, place=None, across=None, halos=None):
     depth, rows, columns = density.shape
     wide = 64
     depth_total = depth * wide
     if place is None:
         place = lambda: lax.axis_index("wide")
+        across = lambda: lax.axis_index("narrow")
     f32 = jnp.float32
     vmem = pl.BlockSpec(memory_space=pltpu.VMEM)
     smem = pl.BlockSpec(memory_space=pltpu.SMEM)
     if halos is None:
-        up_wide = [(i, i + 1) for i in range(wide - 1)]
-        down_wide = [(b, a) for a, b in up_wide]
-        up_narrow = [(i, i + 1) for i in range(7)]
-        down_narrow = [(b, a) for a, b in up_narrow]
-        lo = lax.ppermute(density[-1], "wide", up_wide)
-        hi = lax.ppermute(density[0], "wide", down_wide)
-        dn = lax.ppermute(density[:, -1], "narrow", up_narrow)
-        up = lax.ppermute(density[:, 0], "narrow", down_narrow)
+        wide_odd = (lax.axis_index("wide") & 1) == 1
+        narrow_odd = (lax.axis_index("narrow") & 1) == 1
+        first, last = density[:, 0], density[:, -1]
+        row_a = lax.ppermute(jnp.where(narrow_odd, first, last), "narrow", pairs(8, 0))
+        row_b = lax.ppermute(jnp.where(narrow_odd, last, first), "narrow", pairs(8, 1))
+        first, last = density[0], density[-1]
+        slice_a = lax.ppermute(jnp.where(wide_odd, first, last), "wide", pairs(wide, 0))
+        slice_b = lax.ppermute(jnp.where(wide_odd, last, first), "wide", pairs(wide, 1))
     else:
-        lo, hi, dn, up = halos
+        slice_a, slice_b, row_a, row_b = halos
     slab = (depth, rows, columns)
     wider = (depth, rows, columns + LANES)
     widest = (depth, rows, columns + (LEFT + RIGHT) * LANES)
@@ -303,17 +341,17 @@
         compiler_params=pltpu.CompilerParams(vmem_limit_bytes=LIMIT),
         cost_estimate=pl.CostEstimate(flops=30_000_000, bytes_accessed=10_000_000, transcendentals=0),
         name="lookup",
-    )(view_shear, density, color_table, opacity_table[None])
+    )(view_shear, density, color_table, opacity_table)
     bricks = pl.pallas_call(
-        functools.partial(shade_kernel, depth_total=depth_total, place=place),
+        functools.partial(shade_kernel, depth_total=depth_total, place=place, across=across),
         in_specs=[smem] + [vmem] * 11,
         out_specs=vmem,
-        out_shape=jax.ShapeDtypeStruct((wide, rows, LANES), f32),
+        out_shape=pltpu.VMEM((wide, rows, LANES), jnp.int16),
         scratch_shapes=[pltpu.VMEM(widest, f32), pltpu.VMEM(wider, f32), pltpu.VMEM((depth, columns), f32),
                         pltpu.VMEM((depth, columns), f32), pltpu.VMEM((3,) + row, f32), pltpu.VMEM((3,) + row, f32)],
         compiler_params=pltpu.CompilerParams(vmem_limit_bytes=LIMIT),
         name="shade",
-    )(view_shear, *local, lo, hi, dn, up)
+    )(view_shear, *local, slice_a, slice_b, row_a, row_b)
     if halos is not None:
         return bricks
     parts = lax.all_to_all(bricks, "wide", split_axis=0, concat_axis=0, tiled=True)

time: 72.5 us -> 63.5 us (0.88)
  blocking collectives: 42.7 us -> 34.6 us
  Pallas kernels: 13.5 us -> 11.7 us
  starting transfers between devices: 11.4 us -> 12.4 us
  local copies, waits for them, and re-layouts: 3.68 us -> 2.8 us
  other arithmetic: 0 us -> 0.87 us
    all_to_all x1, blocking collectives: 42.7 us -> 34.6 us  [per_device(): lax.all_to_all(bricks, 'wide', split_axis=0, concat_axis=0, tiled=True)]
    pallas_call x1, Pallas kernels: 8.92 us -> 7.08 us  [per_device(): pl.pallas_call(functools.partial(lookup_kernel, depth_total=depth_total,...]
    ppermute x4, starting transfers between devices: 11.4 us -> 12.4 us  [the longest x1 6.31 us: per_device(): lax.ppermute(jnp.where(wide_odd, first, last), 'wide', pairs(wide, 0))]
    select_n x0 -> x2, other arithmetic: none -> 0.87 us  [the longest x1 0.79 us: per_device(): jnp.where(wide_odd, last, first)]
    squeeze x1 -> x0, local copies, waits for them, and re-layouts: 0.78 us -> none  [per_device(): hi = lax.ppermute(density[0], 'wide', down_wide)]
  transfers between devices with their start and end apart: 4 -> 4, of which waited for: 0 -> 0; matrix products, arithmetic and copies ran while one was open for 2% -> 1% of each run, Pallas kernels for 12% -> 11%
where the time goes in v2:
time: 63.5 us; the launch traced here: 63.1 us
  blocking collectives  34.6 us (54%)
  starting transfers between devices  12.4 us (20%)
  Pallas kernels  11.7 us (18%)
  local copies, waits for them, and re-layouts  2.8 us (4%)
  other arithmetic  0.87 us (1%)
  between operations  0.76 us (1%)
    all_to_all x1, blocking collectives, per_device(): lax.all_to_all(bricks, 'wide', split_axis=0, concat_axis=0, tiled=True)  34.6 us
    pallas_call x1, Pallas kernels, per_device(): pl.pallas_call(functools.partial(lookup_kernel, depth_total=depth_total,...  7.08 us
    ppermute x1, starting transfers between devices, per_device(): lax.ppermute(jnp.where(wide_odd, first, last), 'wide', pairs(wide, 0))  6.31 us
    ppermute x1, starting transfers between devices, per_device(): lax.ppermute(jnp.where(narrow_odd, first, last), 'narrow', pairs(8, 0))  3.5 us
    pallas_call x1, Pallas kernels, per_device(): pl.pallas_call(functools.partial(shade_kernel, depth_total=depth_total, p...  2.77 us
    ppermute x1, starting transfers between devices, per_device(): lax.ppermute(jnp.where(narrow_odd, last, first), 'narrow', pairs(8, 1))  1.92 us
    pallas_call x1, Pallas kernels, per_device(): pl.pallas_call(merge_kernel, in_specs=[smem, vmem], out_specs=vmem, out_s...  1.81 us
    slice x1, local copies, waits for them, and re-layouts, per_device(): first, last = (density[:, 0], density[:, -1])  1.46 us
  transfers between devices with their start and end apart: 4, of which 0 were waited for; matrix products, arithmetic and copies ran while one was open for 1% of the time, Pallas kernels for 11%

profile of v2, /device:TPU:2, one launch (start us, length us, event | category | flops | bytes accessed | tf_op | source)
XLA Modules:
  0.0 63.1 jit_solution(1499593103187460359)
XLA Ops:
  0.0 0.0 copy-start
  0.0 1.5 %fusion = (bf16[16,1,2048]{2,1,0:T(2,128)(2,1)S(1)}, bf16[16,1,2048]{2,1,0:T(2,128)(2,1)S(1)}) fusion(bf16[16,8,2048]{2,1,0:T(8,128)(2,1)} %dens_ref.1), kind=kLoop, calls=%fused_computation.4 | loop fusion | bytes 262144 | tf_op jit(solution)/shard_map/slice | solution.py:322
  1.5 0.1 select_bitcast_fusion
  1.6 1.9 %collective-permute-start.3 = (bf16[16,2048]{1,0:T(8,128)(2,1)S(1)}, bf16[16,2048]{1,0:T(8,128)(2,1)S(1)}, u32[]{:S(2)}, u32[]{:S(2)}) collective-permute-start(bf16[16,2048]{1,0:T(8,128)(2,1)S(1)} %get-tuple-element.23), channel_id=1, source_target_pairs={{1,2},{2,1},{3,4},{4,3},{5,6},{6,5},{9,10},{10,9},{11,12},{12,11},... | collective-permute-start | bytes 196616 | tf_op jit(solution)/shard_map/ppermute | solution.py:324
  3.5 3.5 %collective-permute-start.2 = (bf16[16,2048]{1,0:T(8,128)(2,1)S(1)}, bf16[16,2048]{1,0:T(8,128)(2,1)S(1)}, u32[]{:S(2)}, u32[]{:S(2)}) collective-permute-start(bf16[16,2048]{1,0:T(8,128)(2,1)S(1)} %get-tuple-element.24), channel_id=1, source_target_pairs={{0,1},{1,0},{2,3},{3,2},{4,5},{5,4},{6,7},{7,6},{8,9},{9,8},{10,11... | collective-permute-start | bytes 196616 | tf_op jit(solution)/shard_map/ppermute | solution.py:323
  7.0 0.8 %select_bitcast_fusion.2 = (bf16[8,2048]{1,0:T(8,128)(2,1)S(1)}, bf16[8,2048]{1,0:T(8,128)(2,1)S(1)}) fusion(pred[]{:T(512)S(6)} %eq.6, bf16[16,8,2048]{2,1,0:T(8,128)(2,1)} %dens_ref.1), kind=kLoop, calls=%fused_computation.2 | loop fusion | flops 32768 | bytes 131073 | tf_op jit(solution)/shard_map/jit(_where)/select_n | solution.py:327
  7.8 0.7 %collective-permute-start.1 = (bf16[8,2048]{1,0:T(8,128)(2,1)S(1)}, bf16[8,2048]{1,0:T(8,128)(2,1)S(1)}, u32[]{:S(2)}, u32[]{:S(2)}) collective-permute-start(bf16[8,2048]{1,0:T(8,128)(2,1)S(1)} %get-tuple-element.21), channel_id=1, source_target_pairs={{8,16},{16,8},{24,32},{32,24},{40,48},{48,40},{56,64},{64,56},{72,... | collective-permute-start | bytes 98312 | tf_op jit(solution)/shard_map/ppermute | solution.py:327
  8.5 6.3 %collective-permute-start = (bf16[8,2048]{1,0:T(8,128)(2,1)S(1)}, bf16[8,2048]{1,0:T(8,128)(2,1)S(1)}, u32[]{:S(2)}, u32[]{:S(2)}) collective-permute-start(bf16[8,2048]{1,0:T(8,128)(2,1)S(1)} %get-tuple-element.22), channel_id=1, source_target_pairs={{0,8},{8,0},{16,24},{24,16},{32,40},{40,32},{48,56},{56,48},{64,72... | collective-permute-start | bytes 98312 | tf_op jit(solution)/shard_map/ppermute | solution.py:326
  15.4 0.0 copy-done
  15.4 0.0 copy-start.1
  15.4 0.7 %copy-done.1 = bf16[3,256]{1,0:T(4,128)(2,1)S(1)} copy-done((bf16[3,256]{1,0:T(4,128)(2,1)S(1)}, bf16[3,256]{1,0:T(4,128)(2,1)}, u32[]{:S(2)}) %copy-start.1) | copy-done | bytes 1560
  16.1 0.0 copy-start.2
  16.1 0.7 %copy-done.2 = bf16[256]{0:T(256)(128)(2,1)S(1)} copy-done((bf16[256]{0:T(256)(128)(2,1)S(1)}, bf16[256]{0:T(256)(128)(2,1)}, u32[]{:S(2)}) %copy-start.2) | copy-done | bytes 536
  16.8 7.1 %lookup.1 = (f32[3,16,8,2176]{3,2,1,0:T(8,128)S(1)}, f32[16,8,2176]{2,1,0:T(8,128)S(1)}, f32[16,8,2176]{2,1,0:T(8,128)S(1)}, f32[8,2176]{1,0:T(8,128)S(1)}, f32[...) custom-call(s32[1]{0:T(128)S(6)} %copy.13.shear_ref, ...), custom_call_target="tpu_custom_call" | custom-call | flops 30000000 | bytes 10000000 | tf_op jit(solution)/shard_map/lookup/pallas_call | solution.py:334
  23.9 0.0 collective-permute-done.1.slice_b_ref
  23.9 0.0 collective-permute-done.slice_a_ref
  23.9 0.0 collective-permute-done.3.row_b_ref
  23.9 0.0 collective-permute-done.2.row_a_ref
  23.9 2.8 %shade.1 = s16[64,8,128]{2,1,0:T(8,128)(2,1)S(1)} custom-call(s32[1]{0:T(128)S(6)} %copy.13.shear_ref, f32[3,16,8,2176]{3,2,1,0:T(8,128)S(1)} %get-tuple-element.12.sample_ref, f32[16,8,2176]{2,1,0:T(8,128)S(1)} %get-tuple-element.13.front_ref, f32[16,8,2176]{2,1,0:T(8,128)S(1)} %get-tuple-element.14.back_ref, f32[8,2176]{1,0:T(8,128)S(1)} %get-tuple-element.15.alpha_ref, ...), custom_call_target="tpu_custom_call" | custom-call | tf_op jit(solution)/shard_map/shade/pallas_call | solution.py:345
  26.7 34.6 %all_to_all.5.parts_ref = s16[64,8,128]{2,1,0:T(8,128)(2,1)} all-to-all(s16[64,8,128]{2,1,0:T(8,128)(2,1)S(1)} %shade.1), channel_id=1, replica_groups=mesh['wide'=64,'narrow'=8] {'wide'}, dimensions={0} | all-to-all | bytes 262144 | tf_op jit(solution)/shard_map/all_to_all | solution.py:357
  61.3 1.8 %merge.1 = f32[4,8,32]{2,1,0:T(8,128)} custom-call(s32[1]{0:T(128)S(6)} %copy.13.shear_ref, s16[64,8,128]{2,1,0:T(8,128)(2,1)} %all_to_all.5.parts_ref), custom_call_target="tpu_custom_call" | custom-call | tf_op jit(solution)/shard_map/merge/pallas_call | solution.py:358
Async XLA Ops:
  0.0 15.4 %copy-start = (bf16[16,8,2048]{2,1,0:T(8,128)(2,1)S(1)}, bf16[16,8,2048]{2,1,0:T(8,128)(2,1)}, u32[]{:S(2)}) copy-start(bf16[16,8,2048]{2,1,0:T(8,128)(2,1)} %dens_ref.1) | copy-start | bytes 1572868
  1.6 22.3 %collective-permute-start.3 = (bf16[16,2048]{1,0:T(8,128)(2,1)S(1)}, bf16[16,2048]{1,0:T(8,128)(2,1)S(1)}, u32[]{:S(2)}, u32[]{:S(2)}) collective-permute-start(bf16[16,2048]{1,0:T(8,128)(2,1)S(1)} %get-tuple-element.23), channel_id=1, source_target_pairs={{1,2},{2,1},{3,4},{4,3},{5,6},{6,5},{9,10},{10,9},{11,12},{12,11},... | collective-permute-start | bytes 196616 | tf_op jit(solution)/shard_map/ppermute | solution.py:324
  3.5 20.4 %collective-permute-start.2 = (bf16[16,2048]{1,0:T(8,128)(2,1)S(1)}, bf16[16,2048]{1,0:T(8,128)(2,1)S(1)}, u32[]{:S(2)}, u32[]{:S(2)}) collective-permute-start(bf16[16,2048]{1,0:T(8,128)(2,1)S(1)} %get-tuple-element.24), channel_id=1, source_target_pairs={{0,1},{1,0},{2,3},{3,2},{4,5},{5,4},{6,7},{7,6},{8,9},{9,8},{10,11... | collective-permute-start | bytes 196616 | tf_op jit(solution)/shard_map/ppermute | solution.py:323
  7.8 16.1 %collective-permute-start.1 = (bf16[8,2048]{1,0:T(8,128)(2,1)S(1)}, bf16[8,2048]{1,0:T(8,128)(2,1)S(1)}, u32[]{:S(2)}, u32[]{:S(2)}) collective-permute-start(bf16[8,2048]{1,0:T(8,128)(2,1)S(1)} %get-tuple-element.21), channel_id=1, source_target_pairs={{8,16},{16,8},{24,32},{32,24},{40,48},{48,40},{56,64},{64,56},{72,... | collective-permute-start | bytes 98312 | tf_op jit(solution)/shard_map/ppermute | solution.py:327
  8.5 15.4 %collective-permute-start = (bf16[8,2048]{1,0:T(8,128)(2,1)S(1)}, bf16[8,2048]{1,0:T(8,128)(2,1)S(1)}, u32[]{:S(2)}, u32[]{:S(2)}) collective-permute-start(bf16[8,2048]{1,0:T(8,128)(2,1)S(1)} %get-tuple-element.22), channel_id=1, source_target_pairs={{0,8},{8,0},{16,24},{24,16},{32,40},{40,32},{48,56},{56,48},{64,72... | collective-permute-start | bytes 98312 | tf_op jit(solution)/shard_map/ppermute | solution.py:326
  15.4 0.7 %copy-start.1 = (bf16[3,256]{1,0:T(4,128)(2,1)S(1)}, bf16[3,256]{1,0:T(4,128)(2,1)}, u32[]{:S(2)}) copy-start(bf16[3,256]{1,0:T(4,128)(2,1)} %color_ref.1) | copy-start | bytes 4612
  16.1 0.7 %copy-start.2 = (bf16[256]{0:T(256)(128)(2,1)S(1)}, bf16[256]{0:T(256)(128)(2,1)}, u32[]{:S(2)}) copy-start(bf16[256]{0:T(256)(128)(2,1)} %opacity_ref.1) | copy-start | bytes 1540

commit v3 on v2

--- a/solution.py
+++ b/solution.py
@@ -17,6 +17,8 @@
 LOG_SPAN = 26.0
 LOG_STEPS = 65534.0 / (LOG_SPAN - 1.85)
 TINY = 1e-12
+TURN = 36
+CHUNKS = 4
 LIMIT = 12 * 1024 * 1024
 
 
@@ -74,10 +76,43 @@
     return alpha, alpha * jnp.where(lanes < 96, value * (1.0 / RATIO_STEPS), 1.0)
 
 
-def lookup_kernel(shear_ref, dens_ref, color_ref, opacity_ref,
+def prepare_kernel(dens_hbm, field_ref, slice_a_ref, slice_b_ref, row_a_ref, row_b_ref,
+                   dens_ref, top_ref, bottom_ref, arrived, *, place, across):
+    depth, rows, columns = dens_ref.shape
+    tiles = columns // LANES
+    chunk = depth // CHUNKS
+    copies = [pltpu.make_async_copy(dens_hbm.at[pl.ds(i * chunk, chunk)], dens_ref.at[pl.ds(i * chunk, chunk)],
+                                    arrived.at[i]) for i in range(CHUNKS)]
+    for copy in copies:
+        copy.start()
+    outside = jnp.full((8, LANES), OUTSIDE, jnp.float32)
+    for z in range(depth):
+        for t in range(LEFT):
+            field_ref[z, :, tile(t)] = outside
+        for t in range(RIGHT):
+            field_ref[z, :, tile(LEFT + tiles + t)] = outside
+    for i in range(CHUNKS):
+        copies[i].wait()
+        for z in range(i * chunk, (i + 1) * chunk):
+            slab = dens_ref[z].astype(jnp.float32)
+            field_ref[z, :, pl.ds(LEFT * LANES, columns)] = slab
+            top_ref[z:z + 1, :] = slab[:1]
+            bottom_ref[z:z + 1, :] = slab[rows - 1:]
+    wide_odd = (place() & 1) == 1
+    narrow_odd = (across() & 1) == 1
+    top, bottom = top_ref[...], bottom_ref[...]
+    row_a_ref[...] = jnp.where(narrow_odd, top, bottom).astype(jnp.bfloat16)
+    row_b_ref[...] = jnp.where(narrow_odd, bottom, top).astype(jnp.bfloat16)
+    first = field_ref[0, :, pl.ds(LEFT * LANES, columns)]
+    last = field_ref[depth - 1, :, pl.ds(LEFT * LANES, columns)]
+    slice_a_ref[...] = jnp.where(wide_odd, first, last).astype(jnp.bfloat16)
+    slice_b_ref[...] = jnp.where(wide_odd, last, first).astype(jnp.bfloat16)
+
+
+def lookup_kernel(shear_ref, field_ref, color_hbm, opacity_hbm,
                   sample_ref, front_ref, back_ref, alpha_ref, across_ref, deep_ref, down_ref,
-                  field_ref, value_ref, opaque_ref, ahead_ref, *, depth_total, place):
-    depth, rows, columns = dens_ref.shape
+                  value_ref, opaque_ref, ahead_ref, color_ref, opacity_ref, arrived, *, depth_total, place):
+    depth, rows, columns = across_ref.shape
     tiles = columns // LANES
     lanes = lane_ids()
     rows8 = row_ids()
@@ -85,17 +120,10 @@
     start = place() * depth
     flip = (shear & 1) == 1
     zero = jnp.zeros((8, LANES), jnp.float32)
-    outside = jnp.full((8, LANES), OUTSIDE, jnp.float32)
-
-    def widen(z, carry):
-        for t in range(LEFT):
-            field_ref[z, :, tile(t)] = outside
-        for t in range(RIGHT):
-            field_ref[z, :, tile(LEFT + tiles + t)] = outside
-        field_ref[z, :, pl.ds(LEFT * LANES, columns)] = dens_ref[z].astype(jnp.float32)
-        return carry
-
-    lax.fori_loop(0, depth, widen, 0)
+    copies = [pltpu.make_async_copy(color_hbm, color_ref, arrived.at[0]),
+              pltpu.make_async_copy(opacity_hbm, opacity_ref, arrived.at[1])]
+    for copy in copies:
+        copy.start()
 
     def align(i, carry):
         for j in range(UNROLL):
@@ -111,6 +139,8 @@
 
     lax.fori_loop(0, depth // UNROLL, align, 0)
 
+    for copy in copies:
+        copy.wait()
     evens, odds = [], []
     half = (2 * lanes) & 127
     low = lanes < 64
@@ -121,7 +151,41 @@
         evens.append(jnp.where(low, pick(first, half), pick(second, half)))
         odds.append(jnp.where(low, pick(first, half + 1), pick(second, half + 1)))
 
+    def slopes(z):
+        if True:
+            before = lax.max(z - 1, 0)
+            after = lax.min(z + 1, depth - 1)
+            inner_low = jnp.where(z > 0, 1.0, 0.0)
+            inner_high = jnp.where(z < depth - 1, 1.0, 0.0)
+            slabs = [field_ref[z, :, tile(LEFT + t)] for t in range(tiles)]
+            later = [zero] + [pltpu.roll(v, 1, 1) for v in slabs]
+            sooner = [pltpu.roll(v, LANES - 1, 1) for v in slabs] + [zero]
+            for t in range(tiles):
+                left = jnp.where(lanes == 0, later[t], later[t + 1])
+                right = jnp.where(lanes == LANES - 1, sooner[t + 1], sooner[t])
+                below = jnp.where(rows8 == 7, 0.0, pltpu.roll(slabs[t], 7, 0))
+                above = jnp.where(rows8 == 0, 0.0, pltpu.roll(slabs[t], 1, 0))
+                across_ref[z, :, tile(t)] = right - left
+                down_ref[z, :, tile(t)] = below - above
+                deep_ref[z, :, tile(t)] = (inner_high * field_ref[after, :, tile(LEFT + t)]
+                                           - inner_low * field_ref[before, :, tile(LEFT + t)])
+
+    evens = [(jnp.floor(evens[0] * 32767.0 + 0.5).astype(jnp.int32) * 65536
+              + jnp.floor(evens[1] * 65535.0 + 0.5).astype(jnp.int32)), evens[3] + evens[3] * (evens[2] * (1.0 / 512.0))]
+    odds = [(jnp.floor(odds[0] * 32767.0 + 0.5).astype(jnp.int32) * 65536
+             + jnp.floor(odds[1] * 65535.0 + 0.5).astype(jnp.int32)), odds[3] + odds[3] * (odds[2] * (1.0 / 512.0))]
+
+    def split(word):
+        return [lax.shift_right_logical(word, 16).astype(jnp.float32), (word & 65535).astype(jnp.float32)]
+
+    def part(word):
+        wide = word * 65537.0
+        opacity = wide - (wide - word)
+        return [(word - opacity) * pl.reciprocal(opacity, approx=True), opacity]
+
     def sample(i, carry):
+        for j in range(FEW):
+            slopes(i * FEW + j)
         for z, t in [(i * FEW + j, t) for j in range(FEW) for t in range(tiles + 1)]:
             value = value_ref[z, :, tile(t)]
             scaled = value * 255.0
@@ -131,10 +195,13 @@
             weight = jnp.abs(scaled - (2 * even).astype(jnp.float32))
             lower = [pick(table, even) for table in evens]
             upper = [pick(table, odd) for table in odds]
+            lower = split(lower[0]) + part(lower[1])
+            upper = split(upper[0]) + part(upper[1])
             mixed = [e + weight * (o - e) for e, o in zip(lower, upper)]
             opacity = jnp.where(value >= 0.0, mixed[3], 0.0)
-            for c in range(3):
-                sample_ref[c, z, :, tile(t)] = mixed[c] * opacity
+            sample_ref[0, z, :, tile(t)] = mixed[0] * (opacity * (1.0 / 32767.0))
+            sample_ref[1, z, :, tile(t)] = mixed[1] * (opacity * (1.0 / 65535.0))
+            sample_ref[2, z, :, tile(t)] = mixed[2] * (opacity * 512.0)
             opaque_ref[z, :, tile(t)] = opacity
         return carry
 
@@ -170,29 +237,6 @@
 
     lax.fori_loop(0, depth // UNROLL, advance, 0)
 
-    def slopes(i, carry):
-        for j in range(UNROLL):
-            z = i * UNROLL + j
-            before = lax.max(z - 1, 0)
-            after = lax.min(z + 1, depth - 1)
-            inner_low = jnp.where(z > 0, 1.0, 0.0)
-            inner_high = jnp.where(z < depth - 1, 1.0, 0.0)
-            slabs = [field_ref[z, :, tile(LEFT + t)] for t in range(tiles)]
-            later = [zero] + [pltpu.roll(v, 1, 1) for v in slabs]
-            sooner = [pltpu.roll(v, LANES - 1, 1) for v in slabs] + [zero]
-            for t in range(tiles):
-                left = jnp.where(lanes == 0, later[t], later[t + 1])
-                right = jnp.where(lanes == LANES - 1, sooner[t + 1], sooner[t])
-                below = jnp.where(rows8 == 7, 0.0, pltpu.roll(slabs[t], 7, 0))
-                above = jnp.where(rows8 == 0, 0.0, pltpu.roll(slabs[t], 1, 0))
-                across_ref[z, :, tile(t)] = right - left
-                down_ref[z, :, tile(t)] = below - above
-                deep_ref[z, :, tile(t)] = (inner_high * field_ref[after, :, tile(LEFT + t)]
-                                           - inner_low * field_ref[before, :, tile(LEFT + t)])
-        return carry
-
-    lax.fori_loop(0, depth // UNROLL, slopes, 0)
-
 
 def shade_kernel(shear_ref, sample_ref, front_ref, back_ref, alpha_ref, across_ref, deep_ref, down_ref,
                  slice_a_ref, slice_b_ref, row_a_ref, row_b_ref,
@@ -283,7 +327,7 @@
             moved = [parts[c] if c == y else pltpu.roll(parts[c], (32 * (c - y)) % LANES, 1) for c in range(4)]
             block = jnp.where(quarter < 2, jnp.where(quarter == 0, moved[0], moved[1]),
                               jnp.where(quarter == 2, moved[2], moved[3]))
-            out_ref[4 * t + y] = block.astype(jnp.int16)
+            out_ref[(4 * t + y - TURN) % (4 * tiles)] = block.astype(jnp.int16)
 
 
 def merge_kernel(shear_ref, parts_ref, out_ref):
@@ -295,7 +339,7 @@
     through = jnp.ones((8, LANES), jnp.float32)
     for i in range(count):
         slot = jnp.where(flip, count - 1 - i, i)
-        alpha, value = decode(parts_ref[slot], lanes, owner, phase(slot))
+        alpha, value = decode(parts_ref[(slot - TURN) & (count - 1)], lanes, owner, phase(slot))
         total = total + through * value
         through = through - through * alpha
     for c in range(4):
@@ -316,32 +360,43 @@
     f32 = jnp.float32
     vmem = pl.BlockSpec(memory_space=pltpu.VMEM)
     smem = pl.BlockSpec(memory_space=pltpu.SMEM)
-    if halos is None:
-        wide_odd = (lax.axis_index("wide") & 1) == 1
-        narrow_odd = (lax.axis_index("narrow") & 1) == 1
-        first, last = density[:, 0], density[:, -1]
-        row_a = lax.ppermute(jnp.where(narrow_odd, first, last), "narrow", pairs(8, 0))
-        row_b = lax.ppermute(jnp.where(narrow_odd, last, first), "narrow", pairs(8, 1))
-        first, last = density[0], density[-1]
-        slice_a = lax.ppermute(jnp.where(wide_odd, first, last), "wide", pairs(wide, 0))
-        slice_b = lax.ppermute(jnp.where(wide_odd, last, first), "wide", pairs(wide, 1))
-    else:
-        slice_a, slice_b, row_a, row_b = halos
+    hbm = pl.BlockSpec(memory_space=pl.ANY)
     slab = (depth, rows, columns)
     wider = (depth, rows, columns + LANES)
     widest = (depth, rows, columns + (LEFT + RIGHT) * LANES)
     row = (rows, columns + LANES)
+    density, color_table, opacity_table = [pltpu.with_memory_space_constraint(v, pltpu.HBM) for v in (density, color_table, opacity_table)]
+    field, slice_a, slice_b, row_a, row_b = pl.pallas_call(
+        functools.partial(prepare_kernel, place=place, across=across),
+        in_specs=[hbm],
+        out_specs=[vmem] * 5,
+        out_shape=[pltpu.VMEM(widest, f32)] + [pltpu.VMEM((rows, columns), density.dtype)] * 2
+        + [pltpu.VMEM((depth, columns), density.dtype)] * 2,
+        scratch_shapes=[pltpu.VMEM(slab, density.dtype), pltpu.VMEM((depth, columns), f32),
+                        pltpu.VMEM((depth, columns), f32), pltpu.SemaphoreType.DMA((CHUNKS,))],
+        compiler_params=pltpu.CompilerParams(vmem_limit_bytes=LIMIT),
+        name="prepare",
+    )(density)
+    if halos is None:
+        row_a = lax.ppermute(row_a, "narrow", pairs(8, 0))
+        row_b = lax.ppermute(row_b, "narrow", pairs(8, 1))
+        slice_a = lax.ppermute(slice_a, "wide", pairs(wide, 0))
+        slice_b = lax.ppermute(slice_b, "wide", pairs(wide, 1))
+    else:
+        slice_a, slice_b, row_a, row_b = halos
     local = pl.pallas_call(
         functools.partial(lookup_kernel, depth_total=depth_total, place=place),
-        in_specs=[smem, vmem, vmem, vmem],
+        in_specs=[smem, vmem, hbm, hbm],
         out_specs=[vmem] * 7,
         out_shape=[pltpu.VMEM((3,) + wider, f32), pltpu.VMEM(wider, f32), pltpu.VMEM(wider, f32), pltpu.VMEM(row, f32),
                    pltpu.VMEM(slab, f32), pltpu.VMEM(slab, f32), pltpu.VMEM(slab, f32)],
-        scratch_shapes=[pltpu.VMEM(widest, f32), pltpu.VMEM(wider, f32), pltpu.VMEM(wider, f32), pltpu.VMEM(row, f32)],
+        scratch_shapes=[pltpu.VMEM(wider, f32), pltpu.VMEM(wider, f32), pltpu.VMEM(row, f32),
+                        pltpu.VMEM(color_table.shape, color_table.dtype),
+                        pltpu.VMEM(opacity_table.shape, opacity_table.dtype), pltpu.SemaphoreType.DMA((2,))],
         compiler_params=pltpu.CompilerParams(vmem_limit_bytes=LIMIT),
         cost_estimate=pl.CostEstimate(flops=30_000_000, bytes_accessed=10_000_000, transcendentals=0),
         name="lookup",
-    )(view_shear, density, color_table, opacity_table)
+    )(view_shear, field, color_table, opacity_table)
     bricks = pl.pallas_call(
         functools.partial(shade_kernel, depth_total=depth_total, place=place, across=across),
         in_specs=[smem] + [vmem] * 11,
@@ -354,7 +409,8 @@
     )(view_shear, *local, slice_a, slice_b, row_a, row_b)
     if halos is not None:
         return bricks
-    parts = lax.all_to_all(bricks, "wide", split_axis=0, concat_axis=0, tiled=True)
+    order = [(i + TURN) % wide for i in range(wide)]
+    parts = lax.all_to_all(bricks, "wide", split_axis=0, concat_axis=0, axis_index_groups=[order], tiled=True)
     return pl.pallas_call(
         merge_kernel,
         in_specs=[smem, vmem],

time: 63.5 us -> 53.1 us (0.84)
  blocking collectives: 34.6 us -> 28.5 us
  local copies, waits for them, and re-layouts: 2.8 us -> 0 us
  other arithmetic: 0.87 us -> 0 us
    all_to_all x1, blocking collectives: 34.6 us -> 28.5 us  [per_device(): lax.all_to_all(bricks, 'wide', split_axis=0, concat_axis=0, axis_index_gr...]
    pallas_call x1, Pallas kernels: 7.08 us -> 5.36 us  [per_device(): pl.pallas_call(functools.partial(lookup_kernel, depth_total=depth_total,...]
    slice x1 -> x0, local copies, waits for them, and re-layouts: 1.46 us -> none  [per_device(): first, last = (density[:, 0], density[:, -1])]
    unnamed x6 -> x0, local copies, waits for them, and re-layouts: 1.34 us -> none
    pallas_call x0 -> x1, Pallas kernels: none -> 1.2 us  [per_device(): pl.pallas_call(functools.partial(prepare_kernel, place=place, across=acro...]
    select_n x2 -> x0, other arithmetic: 0.87 us -> none  [the longest x1 0.79 us: per_device(): jnp.where(wide_odd, last, first)]
  transfers between devices with their start and end apart: 4 -> 4, of which waited for: 0 -> 0; matrix products, arithmetic and copies ran while one was open for 1% -> 0% of each run, Pallas kernels for 11% -> 10%
where the time goes in v3:
time: 53.1 us; the launch traced here: 52.8 us
  blocking collectives  28.5 us (54%)
  starting transfers between devices  12.4 us (23%)
  Pallas kernels  11.2 us (21%)
  between operations  0.73 us (1%)
    all_to_all x1, blocking collectives, per_device(): lax.all_to_all(bricks, 'wide', split_axis=0, concat_axis=0, axis_index_gr...  28.5 us
    ppermute x1, starting transfers between devices, per_device(): row_b = lax.ppermute(row_b, 'narrow', pairs(8, 1))  7.92 us
    pallas_call x1, Pallas kernels, per_device(): pl.pallas_call(functools.partial(lookup_kernel, depth_total=depth_total,...  5.36 us
    pallas_call x1, Pallas kernels, per_device(): pl.pallas_call(functools.partial(shade_kernel, depth_total=depth_total, p...  2.76 us
    ppermute x1, starting transfers between devices, per_device(): row_a = lax.ppermute(row_a, 'narrow', pairs(8, 0))  1.92 us
    ppermute x1, starting transfers between devices, per_device(): slice_a = lax.ppermute(slice_a, 'wide', pairs(wide, 0))  1.92 us
    pallas_call x1, Pallas kernels, per_device(): pl.pallas_call(merge_kernel, in_specs=[smem, vmem], out_specs=vmem, out_s...  1.85 us
    pallas_call x1, Pallas kernels, per_device(): pl.pallas_call(functools.partial(prepare_kernel, place=place, across=acro...  1.2 us
  transfers between devices with their start and end apart: 4, of which 0 were waited for; matrix products, arithmetic and copies ran while one was open for 0% of the time, Pallas kernels for 10%

profile of v3, /device:TPU:2, one launch (start us, length us, event | category | flops | bytes accessed | tf_op | source)
XLA Modules:
  0.0 52.8 jit_solution(14028338765084058054)
XLA Ops:
  0.0 1.2 %prepare.1 = (f32[16,8,2688]{2,1,0:T(8,128)S(1)}, bf16[8,2048]{1,0:T(8,128)(2,1)S(1)}, bf16[8,2048]{1,0:T(8,128)(2,1)S(1)}, bf16[16,2048]{1,0:T(8,128)(2,1)S(1)}, bf16[16,2048]{1,0:T(8,128)(2,1)S(1)}) custom-call(bf16[16,8,2048]{2,1,0:T(8,128)(2,1)} %dens_hbm.1), custom_call_target="tpu_custom_call" | custom-call | tf_op jit(solution)/shard_map/prepare/pallas_call | solution.py:369
  1.2 1.9 %collective-permute-start.2 = (bf16[16,2048]{1,0:T(8,128)(2,1)S(1)}, bf16[16,2048]{1,0:T(8,128)(2,1)S(1)}, u32[]{:S(2)}, u32[]{:S(2)}) collective-permute-start(bf16[16,2048]{1,0:T(8,128)(2,1)S(1)} %get-tuple-element.27), channel_id=1, source_target_pairs={{0,1},{1,0},{2,3},{3,2},{4,5},{5,4},{6,7},{7,6},{8,9},{9,8},{10,11... | collective-permute-start | bytes 196616 | tf_op jit(solution)/shard_map/ppermute | solution.py:381
  3.1 7.9 %collective-permute-start.3 = (bf16[16,2048]{1,0:T(8,128)(2,1)S(1)}, bf16[16,2048]{1,0:T(8,128)(2,1)S(1)}, u32[]{:S(2)}, u32[]{:S(2)}) collective-permute-start(bf16[16,2048]{1,0:T(8,128)(2,1)S(1)} %get-tuple-element.28), channel_id=1, source_target_pairs={{1,2},{2,1},{3,4},{4,3},{5,6},{6,5},{9,10},{10,9},{11,12},{12,11},... | collective-permute-start | bytes 196616 | tf_op jit(solution)/shard_map/ppermute | solution.py:382
  11.1 1.9 %collective-permute-start = (bf16[8,2048]{1,0:T(8,128)(2,1)S(1)}, bf16[8,2048]{1,0:T(8,128)(2,1)S(1)}, u32[]{:S(2)}, u32[]{:S(2)}) collective-permute-start(bf16[8,2048]{1,0:T(8,128)(2,1)S(1)} %get-tuple-element.25), channel_id=1, source_target_pairs={{0,8},{8,0},{16,24},{24,16},{32,40},{40,32},{48,56},{56,48},{64,72... | collective-permute-start | bytes 98312 | tf_op jit(solution)/shard_map/ppermute | solution.py:383
  13.0 0.7 %collective-permute-start.1 = (bf16[8,2048]{1,0:T(8,128)(2,1)S(1)}, bf16[8,2048]{1,0:T(8,128)(2,1)S(1)}, u32[]{:S(2)}, u32[]{:S(2)}) collective-permute-start(bf16[8,2048]{1,0:T(8,128)(2,1)S(1)} %get-tuple-element.26), channel_id=1, source_target_pairs={{8,16},{16,8},{24,32},{32,24},{40,48},{48,40},{56,64},{64,56},{72,... | collective-permute-start | bytes 98312 | tf_op jit(solution)/shard_map/ppermute | solution.py:384
  14.3 5.4 %lookup.1 = (f32[3,16,8,2176]{3,2,1,0:T(8,128)S(1)}, f32[16,8,2176]{2,1,0:T(8,128)S(1)}, f32[16,8,2176]{2,1,0:T(8,128)S(1)}, f32[8,2176]{1,0:T(8,128)S(1)}, f32[...) custom-call(s32[1]{0:T(128)S(6)} %copy.5.shear_ref, ...), custom_call_target="tpu_custom_call" | custom-call | flops 30000000 | bytes 10000000 | tf_op jit(solution)/shard_map/lookup/pallas_call | solution.py:387
  19.7 0.0 collective-permute-done.slice_a_ref
  19.7 0.0 collective-permute-done.1.slice_b_ref
  19.7 0.0 collective-permute-done.2.row_a_ref
  19.7 0.0 collective-permute-done.3.row_b_ref
  19.7 2.8 %shade.1 = s16[64,8,128]{2,1,0:T(8,128)(2,1)S(1)} custom-call(s32[1]{0:T(128)S(6)} %copy.5.shear_ref, f32[3,16,8,2176]{3,2,1,0:T(8,128)S(1)} %get-tuple-element.18.sample_ref, f32[16,8,2176]{2,1,0:T(8,128)S(1)} %get-tuple-element.19.front_ref, f32[16,8,2176]{2,1,0:T(8,128)S(1)} %get-tuple-element.20.back_ref, f32[8,2176]{1,0:T(8,128)S(1)} %get-tuple-element.21.alpha_ref, ...), custom_call_target="tpu_custom_call" | custom-call | tf_op jit(solution)/shard_map/shade/pallas_call | solution.py:400
  22.5 28.5 %all_to_all.5.parts_ref = s16[64,8,128]{2,1,0:T(8,128)(2,1)} all-to-all(s16[64,8,128]{2,1,0:T(8,128)(2,1)S(1)} %shade.1), channel_id=1, replica_groups={{288,296,304,312,320,328,336,344,352,360,368,376,384,392,400,408,416,42..., dimensions={0} | all-to-all | bytes 262144 | tf_op jit(solution)/shard_map/all_to_all | solution.py:413
  51.0 1.8 %merge.1 = f32[4,8,32]{2,1,0:T(8,128)} custom-call(s32[1]{0:T(128)S(6)} %copy.5.shear_ref, s16[64,8,128]{2,1,0:T(8,128)(2,1)} %all_to_all.5.parts_ref), custom_call_target="tpu_custom_call" | custom-call | tf_op jit(solution)/shard_map/merge/pallas_call | solution.py:414
Async XLA Ops:
  1.2 18.5 %collective-permute-start.2 = (bf16[16,2048]{1,0:T(8,128)(2,1)S(1)}, bf16[16,2048]{1,0:T(8,128)(2,1)S(1)}, u32[]{:S(2)}, u32[]{:S(2)}) collective-permute-start(bf16[16,2048]{1,0:T(8,128)(2,1)S(1)} %get-tuple-element.27), channel_id=1, source_target_pairs={{0,1},{1,0},{2,3},{3,2},{4,5},{5,4},{6,7},{7,6},{8,9},{9,8},{10,11... | collective-permute-start | bytes 196616 | tf_op jit(solution)/shard_map/ppermute | solution.py:381
  3.1 16.6 %collective-permute-start.3 = (bf16[16,2048]{1,0:T(8,128)(2,1)S(1)}, bf16[16,2048]{1,0:T(8,128)(2,1)S(1)}, u32[]{:S(2)}, u32[]{:S(2)}) collective-permute-start(bf16[16,2048]{1,0:T(8,128)(2,1)S(1)} %get-tuple-element.28), channel_id=1, source_target_pairs={{1,2},{2,1},{3,4},{4,3},{5,6},{6,5},{9,10},{10,9},{11,12},{12,11},... | collective-permute-start | bytes 196616 | tf_op jit(solution)/shard_map/ppermute | solution.py:382
  11.1 8.6 %collective-permute-start = (bf16[8,2048]{1,0:T(8,128)(2,1)S(1)}, bf16[8,2048]{1,0:T(8,128)(2,1)S(1)}, u32[]{:S(2)}, u32[]{:S(2)}) collective-permute-start(bf16[8,2048]{1,0:T(8,128)(2,1)S(1)} %get-tuple-element.25), channel_id=1, source_target_pairs={{0,8},{8,0},{16,24},{24,16},{32,40},{40,32},{48,56},{56,48},{64,72... | collective-permute-start | bytes 98312 | tf_op jit(solution)/shard_map/ppermute | solution.py:383
  13.0 6.7 %collective-permute-start.1 = (bf16[8,2048]{1,0:T(8,128)(2,1)S(1)}, bf16[8,2048]{1,0:T(8,128)(2,1)S(1)}, u32[]{:S(2)}, u32[]{:S(2)}) collective-permute-start(bf16[8,2048]{1,0:T(8,128)(2,1)S(1)} %get-tuple-element.26), channel_id=1, source_target_pairs={{8,16},{16,8},{24,32},{32,24},{40,48},{48,40},{56,64},{64,56},{72,... | collective-permute-start | bytes 98312 | tf_op jit(solution)/shard_map/ppermute | solution.py:384

commit v4 on v3

--- a/solution.py
+++ b/solution.py
@@ -10,7 +10,7 @@
 LANES = 128
 LEFT = 3
 RIGHT = 2
-UNROLL = 4
+STEPS = 16
 FEW = 4
 OUTSIDE = -1.0 / 512
 RATIO_STEPS = 65000.0
@@ -76,14 +76,17 @@
     return alpha, alpha * jnp.where(lanes < 96, value * (1.0 / RATIO_STEPS), 1.0)
 
 
-def prepare_kernel(dens_hbm, field_ref, slice_a_ref, slice_b_ref, row_a_ref, row_b_ref,
-                   dens_ref, top_ref, bottom_ref, arrived, *, place, across):
+def prepare_kernel(dens_hbm, color_hbm, opacity_hbm,
+                   field_ref, slice_a_ref, slice_b_ref, row_a_ref, row_b_ref, pair_ref, mixed_ref,
+                   dens_ref, top_ref, bottom_ref, color_ref, opacity_ref, arrived, *, place, across):
     depth, rows, columns = dens_ref.shape
     tiles = columns // LANES
     chunk = depth // CHUNKS
     copies = [pltpu.make_async_copy(dens_hbm.at[pl.ds(i * chunk, chunk)], dens_ref.at[pl.ds(i * chunk, chunk)],
                                     arrived.at[i]) for i in range(CHUNKS)]
-    for copy in copies:
+    tables = [pltpu.make_async_copy(color_hbm, color_ref, arrived.at[CHUNKS]),
+              pltpu.make_async_copy(opacity_hbm, opacity_ref, arrived.at[CHUNKS + 1])]
+    for copy in copies + tables:
         copy.start()
     outside = jnp.full((8, LANES), OUTSIDE, jnp.float32)
     for z in range(depth):
@@ -91,6 +94,20 @@
             field_ref[z, :, tile(t)] = outside
         for t in range(RIGHT):
             field_ref[z, :, tile(LEFT + tiles + t)] = outside
+    for copy in tables:
+        copy.wait()
+    lanes = lane_ids()
+    half = (2 * lanes) & 127
+    low = lanes < 64
+    rows_of = [color_ref[c:c + 1, :] for c in range(3)] + [opacity_ref[...].reshape(1, -1)]
+    for i in range(2):
+        red, green, blue, opacity = [
+            jnp.where(low, pick(jnp.broadcast_to(row[:, :LANES], (8, LANES)), half + i),
+                      pick(jnp.broadcast_to(row[:, LANES:], (8, LANES)), half + i))
+            for row in [r.astype(jnp.float32) for r in rows_of]]
+        pair_ref[i] = (jnp.floor(red * 32767.0 + 0.5).astype(jnp.int32) * 65536
+                       + jnp.floor(green * 65535.0 + 0.5).astype(jnp.int32))
+        mixed_ref[i] = opacity + opacity * (blue * (1.0 / 512.0))
     for i in range(CHUNKS):
         copies[i].wait()
         for z in range(i * chunk, (i + 1) * chunk):
@@ -109,9 +126,9 @@
     slice_b_ref[...] = jnp.where(wide_odd, last, first).astype(jnp.bfloat16)
 
 
-def lookup_kernel(shear_ref, field_ref, color_hbm, opacity_hbm,
+def lookup_kernel(shear_ref, field_ref, pair_ref, mixed_ref,
                   sample_ref, front_ref, back_ref, alpha_ref, across_ref, deep_ref, down_ref,
-                  value_ref, opaque_ref, ahead_ref, color_ref, opacity_ref, arrived, *, depth_total, place):
+                  opaque_ref, ahead_ref, *, depth_total, place):
     depth, rows, columns = across_ref.shape
     tiles = columns // LANES
     lanes = lane_ids()
@@ -120,37 +137,6 @@
     start = place() * depth
     flip = (shear & 1) == 1
     zero = jnp.zeros((8, LANES), jnp.float32)
-    copies = [pltpu.make_async_copy(color_hbm, color_ref, arrived.at[0]),
-              pltpu.make_async_copy(opacity_hbm, opacity_ref, arrived.at[1])]
-    for copy in copies:
-        copy.start()
-
-    def align(i, carry):
-        for j in range(UNROLL):
-            z = i * UNROLL + j
-            whole, g = shift_of(shear, start + z, depth_total)
-            hop, r = split_shift(whole)
-            base = pl.multiple_of((1 - hop) * LANES, LANES)
-            keep = lanes >= r
-            rolled = [pltpu.roll(field_ref[z, :, pl.ds(base + t * LANES, LANES)], r, 1) for t in range(tiles + 2)]
-            for t in range(tiles + 1):
-                value_ref[z, :, tile(t)] = jnp.where(keep, rolled[t + 1], rolled[t])
-        return carry
-
-    lax.fori_loop(0, depth // UNROLL, align, 0)
-
-    for copy in copies:
-        copy.wait()
-    evens, odds = [], []
-    half = (2 * lanes) & 127
-    low = lanes < 64
-    for c in range(4):
-        row = (color_ref[c:c + 1, :] if c < 3 else opacity_ref[...].reshape(1, -1)).astype(jnp.float32)
-        first = jnp.broadcast_to(row[:, :LANES], (8, LANES))
-        second = jnp.broadcast_to(row[:, LANES:], (8, LANES))
-        evens.append(jnp.where(low, pick(first, half), pick(second, half)))
-        odds.append(jnp.where(low, pick(first, half + 1), pick(second, half + 1)))
-
     def slopes(z):
         if True:
             before = lax.max(z - 1, 0)
@@ -170,10 +156,7 @@
                 deep_ref[z, :, tile(t)] = (inner_high * field_ref[after, :, tile(LEFT + t)]
                                            - inner_low * field_ref[before, :, tile(LEFT + t)])
 
-    evens = [(jnp.floor(evens[0] * 32767.0 + 0.5).astype(jnp.int32) * 65536
-              + jnp.floor(evens[1] * 65535.0 + 0.5).astype(jnp.int32)), evens[3] + evens[3] * (evens[2] * (1.0 / 512.0))]
-    odds = [(jnp.floor(odds[0] * 32767.0 + 0.5).astype(jnp.int32) * 65536
-             + jnp.floor(odds[1] * 65535.0 + 0.5).astype(jnp.int32)), odds[3] + odds[3] * (odds[2] * (1.0 / 512.0))]
+    evens, odds = [[pair_ref[i], mixed_ref[i]] for i in range(2)]
 
     def split(word):
         return [lax.shift_right_logical(word, 16).astype(jnp.float32), (word & 65535).astype(jnp.float32)]
@@ -181,13 +164,24 @@
     def part(word):
         wide = word * 65537.0
         opacity = wide - (wide - word)
-        return [(word - opacity) * pl.reciprocal(opacity, approx=True), opacity]
+        return [(word - opacity) * pltpu.reciprocal(opacity, approx=True), opacity]
 
     def sample(i, carry):
         for j in range(FEW):
             slopes(i * FEW + j)
-        for z, t in [(i * FEW + j, t) for j in range(FEW) for t in range(tiles + 1)]:
-            value = value_ref[z, :, tile(t)]
+        values = {}
+        for j in range(FEW):
+            z = i * FEW + j
+            whole, g = shift_of(shear, start + z, depth_total)
+            hop, r = split_shift(whole)
+            base = pl.multiple_of((1 - hop) * LANES, LANES)
+            keep = lanes >= r
+            rolled = [pltpu.roll(field_ref[z, :, pl.ds(base + t * LANES, LANES)], r, 1) for t in range(tiles + 2)]
+            for t in range(tiles + 1):
+                values[j, t] = jnp.where(keep, rolled[t + 1], rolled[t])
+        for j, t in [(j, t) for j in range(FEW) for t in range(tiles + 1)]:
+            z = i * FEW + j
+            value = values[j, t]
             scaled = value * 255.0
             level = jnp.minimum(scaled.astype(jnp.int32), 254)
             even = lax.shift_right_logical(level + 1, 1)
@@ -212,30 +206,43 @@
         ahead_ref[:, tile(t)] = zero
 
     def advance(i, carry):
-        for j in range(UNROLL):
-            step = i * UNROLL + j
-            z = jnp.where(flip, depth - 1 - step, step)
-            whole, g = shift_of(shear, start + z, depth_total)
-            opaque = [opaque_ref[z, :, tile(t)] for t in range(tiles + 1)]
-            later = [pltpu.roll(v, 1, 1) for v in opaque]
-            sooner = [pltpu.roll(v, LANES - 1, 1) for v in opaque] + [zero]
-            for t in range(tiles + 1):
-                right = jnp.where(lanes == LANES - 1, sooner[t + 1], sooner[t])
-                ahead = ahead_ref[:, tile(t)]
+        places, parts = [], []
+        for j in range(STEPS):
+            step = i * STEPS + j
+            places.append(jnp.where(flip, depth - 1 - step, step))
+            parts.append(shift_of(shear, start + places[j], depth_total)[1])
+        here = [opaque_ref[z, :, tile(0)] for z in places]
+        later = [None] * STEPS
+        sooner = [pltpu.roll(v, LANES - 1, 1) for v in here]
+        for t in range(tiles + 1):
+            ahead = ahead_ref[:, tile(t)]
+            alpha = alpha_ref[:, tile(t)]
+            for j in range(STEPS):
+                z, g, opaque = places[j], parts[j], here[j]
+                if t < tiles:
+                    here[j] = opaque_ref[z, :, tile(t + 1)]
+                    follow = pltpu.roll(here[j], LANES - 1, 1)
+                    right = jnp.where(lanes == LANES - 1, follow, sooner[j])
+                    sooner[j] = follow
+                else:
+                    right = sooner[j]
                 through = 1.0 - ahead
                 front_ref[z, :, tile(t)] = g * through
-                ahead_ref[:, tile(t)] = ahead + through * (right + g * (opaque[t] - right))
+                ahead = ahead + through * (right + g * (opaque - right))
+                behind = pltpu.roll(opaque, 1, 1)
                 if t:
-                    left = jnp.where(lanes == 0, later[t - 1], later[t])
-                    alpha = alpha_ref[:, tile(t)]
+                    left = jnp.where(lanes == 0, later[j], behind)
                     through = 1.0 - alpha
                     back_ref[z, :, tile(t)] = through - g * through
-                    alpha_ref[:, tile(t)] = alpha + through * (opaque[t] + g * (left - opaque[t]))
+                    alpha = alpha + through * (opaque + g * (left - opaque))
                 else:
                     back_ref[z, :, tile(t)] = zero
+                later[j] = behind
+            ahead_ref[:, tile(t)] = ahead
+            alpha_ref[:, tile(t)] = alpha
         return carry
 
-    lax.fori_loop(0, depth // UNROLL, advance, 0)
+    lax.fori_loop(0, depth // STEPS, advance, 0)
 
 
 def shade_kernel(shear_ref, sample_ref, front_ref, back_ref, alpha_ref, across_ref, deep_ref, down_ref,
@@ -286,8 +293,8 @@
     lax.fori_loop(0, tiles, shade, 0)
 
     def align(i, carry):
-        for j in range(UNROLL):
-            z = i * UNROLL + j
+        for j in range(STEPS):
+            z = i * STEPS + j
             whole, g = shift_of(shear, start + z, depth_total)
             hop, r = split_shift(whole)
             base = pl.multiple_of((1 - hop) * LANES, LANES)
@@ -297,7 +304,7 @@
                 moved_ref[z, :, tile(t)] = jnp.where(keep, rolled[t + 1], rolled[t])
         return carry
 
-    lax.fori_loop(0, depth // UNROLL, align, 0)
+    lax.fori_loop(0, depth // STEPS, align, 0)
 
     def gather(t, carry):
         here = pl.ds(pl.multiple_of(t * LANES, LANES), LANES)
@@ -366,17 +373,19 @@
     widest = (depth, rows, columns + (LEFT + RIGHT) * LANES)
     row = (rows, columns + LANES)
     density, color_table, opacity_table = [pltpu.with_memory_space_constraint(v, pltpu.HBM) for v in (density, color_table, opacity_table)]
-    field, slice_a, slice_b, row_a, row_b = pl.pallas_call(
+    field, slice_a, slice_b, row_a, row_b, pair, mixed = pl.pallas_call(
         functools.partial(prepare_kernel, place=place, across=across),
-        in_specs=[hbm],
-        out_specs=[vmem] * 5,
+        in_specs=[hbm] * 3,
+        out_specs=[vmem] * 7,
         out_shape=[pltpu.VMEM(widest, f32)] + [pltpu.VMEM((rows, columns), density.dtype)] * 2
-        + [pltpu.VMEM((depth, columns), density.dtype)] * 2,
+        + [pltpu.VMEM((depth, columns), density.dtype)] * 2
+        + [pltpu.VMEM((2, rows, LANES), jnp.int32), pltpu.VMEM((2, rows, LANES), f32)],
         scratch_shapes=[pltpu.VMEM(slab, density.dtype), pltpu.VMEM((depth, columns), f32),
-                        pltpu.VMEM((depth, columns), f32), pltpu.SemaphoreType.DMA((CHUNKS,))],
+                        pltpu.VMEM((depth, columns), f32), pltpu.VMEM(color_table.shape, color_table.dtype),
+                        pltpu.VMEM(opacity_table.shape, opacity_table.dtype), pltpu.SemaphoreType.DMA((CHUNKS + 2,))],
         compiler_params=pltpu.CompilerParams(vmem_limit_bytes=LIMIT),
         name="prepare",
-    )(density)
+    )(density, color_table, opacity_table)
     if halos is None:
         row_a = lax.ppermute(row_a, "narrow", pairs(8, 0))
         row_b = lax.ppermute(row_b, "narrow", pairs(8, 1))
@@ -386,17 +395,15 @@
         slice_a, slice_b, row_a, row_b = halos
     local = pl.pallas_call(
         functools.partial(lookup_kernel, depth_total=depth_total, place=place),
-        in_specs=[smem, vmem, hbm, hbm],
+        in_specs=[smem, vmem, vmem, vmem],
         out_specs=[vmem] * 7,
         out_shape=[pltpu.VMEM((3,) + wider, f32), pltpu.VMEM(wider, f32), pltpu.VMEM(wider, f32), pltpu.VMEM(row, f32),
                    pltpu.VMEM(slab, f32), pltpu.VMEM(slab, f32), pltpu.VMEM(slab, f32)],
-        scratch_shapes=[pltpu.VMEM(wider, f32), pltpu.VMEM(wider, f32), pltpu.VMEM(row, f32),
-                        pltpu.VMEM(color_table.shape, color_table.dtype),
-                        pltpu.VMEM(opacity_table.shape, opacity_table.dtype), pltpu.SemaphoreType.DMA((2,))],
+        scratch_shapes=[pltpu.VMEM(wider, f32), pltpu.VMEM(row, f32)],
         compiler_params=pltpu.CompilerParams(vmem_limit_bytes=LIMIT),
         cost_estimate=pl.CostEstimate(flops=30_000_000, bytes_accessed=10_000_000, transcendentals=0),
         name="lookup",
-    )(view_shear, field, color_table, opacity_table)
+    )(view_shear, field, pair, mixed)
     bricks = pl.pallas_call(
         functools.partial(shade_kernel, depth_total=depth_total, place=place, across=across),
         in_specs=[smem] + [vmem] * 11,

time: 53.1 us -> 52.2 us (0.983)
  Pallas kernels: 11.2 us -> 10.4 us
    pallas_call x1, Pallas kernels: 5.36 us -> 4.74 us  [per_device(): pl.pallas_call(functools.partial(lookup_kernel, depth_total=depth_total,...]
  transfers between devices with their start and end apart: 4 -> 4, of which waited for: 0 -> 0; matrix products, arithmetic and copies ran while one was open for 0% -> 0% of each run, Pallas kernels for 10% -> 9%
where the time goes in v4:
time: 52.2 us; the launch traced here: 52 us
  blocking collectives  28.5 us (55%)
  starting transfers between devices  12.4 us (24%)
  Pallas kernels  10.4 us (20%)
  between operations  0.73 us (1%)
    all_to_all x1, blocking collectives, per_device(): lax.all_to_all(bricks, 'wide', split_axis=0, concat_axis=0, axis_index_gr...  28.5 us
    ppermute x1, starting transfers between devices, per_device(): row_b = lax.ppermute(row_b, 'narrow', pairs(8, 1))  7.92 us
    pallas_call x1, Pallas kernels, per_device(): pl.pallas_call(functools.partial(lookup_kernel, depth_total=depth_total,...  4.74 us
    pallas_call x1, Pallas kernels, per_device(): pl.pallas_call(functools.partial(shade_kernel, depth_total=depth_total, p...  2.49 us
    ppermute x1, starting transfers between devices, per_device(): row_a = lax.ppermute(row_a, 'narrow', pairs(8, 0))  1.92 us
    ppermute x1, starting transfers between devices, per_device(): slice_a = lax.ppermute(slice_a, 'wide', pairs(wide, 0))  1.92 us
    pallas_call x1, Pallas kernels, per_device(): pl.pallas_call(merge_kernel, in_specs=[smem, vmem], out_specs=vmem, out_s...  1.85 us
    pallas_call x1, Pallas kernels, per_device(): pl.pallas_call(functools.partial(prepare_kernel, place=place, across=acro...  1.29 us
  transfers between devices with their start and end apart: 4, of which 0 were waited for; matrix products, arithmetic and copies ran while one was open for 0% of the time, Pallas kernels for 9%

profile of v4, /device:TPU:2, one launch (start us, length us, event | category | flops | bytes accessed | tf_op | source)
XLA Modules:
  0.0 52.0 jit_solution(843656183248547875)
XLA Ops:
  0.0 1.3 %prepare.1 = (f32[16,8,2688]{2,1,0:T(8,128)S(1)}, bf16[8,2048]{1,0:T(8,128)(2,1)S(1)}, bf16[8,2048]{1,0:T(8,128)(2,1)S(1)}, bf16[16,2048]{1,0:T(8,128)(2,1)S(1)}...) custom-call(bf16[16,8,2048]{2,1,0:T(8,128)(2,1)} %dens_hbm.1, ...), custom_call_target="tpu_custom_call" | custom-call | tf_op jit(solution)/shard_map/prepare/pallas_call | solution.py:376
  1.3 1.9 %collective-permute-start.2 = (bf16[16,2048]{1,0:T(8,128)(2,1)S(1)}, bf16[16,2048]{1,0:T(8,128)(2,1)S(1)}, u32[]{:S(2)}, u32[]{:S(2)}) collective-permute-start(bf16[16,2048]{1,0:T(8,128)(2,1)S(1)} %get-tuple-element.31), channel_id=1, source_target_pairs={{0,1},{1,0},{2,3},{3,2},{4,5},{5,4},{6,7},{7,6},{8,9},{9,8},{10,11... | collective-permute-start | bytes 196616 | tf_op jit(solution)/shard_map/ppermute | solution.py:390
  3.2 7.9 %collective-permute-start.3 = (bf16[16,2048]{1,0:T(8,128)(2,1)S(1)}, bf16[16,2048]{1,0:T(8,128)(2,1)S(1)}, u32[]{:S(2)}, u32[]{:S(2)}) collective-permute-start(bf16[16,2048]{1,0:T(8,128)(2,1)S(1)} %get-tuple-element.32), channel_id=1, source_target_pairs={{1,2},{2,1},{3,4},{4,3},{5,6},{6,5},{9,10},{10,9},{11,12},{12,11},... | collective-permute-start | bytes 196616 | tf_op jit(solution)/shard_map/ppermute | solution.py:391
  11.2 1.9 %collective-permute-start = (bf16[8,2048]{1,0:T(8,128)(2,1)S(1)}, bf16[8,2048]{1,0:T(8,128)(2,1)S(1)}, u32[]{:S(2)}, u32[]{:S(2)}) collective-permute-start(bf16[8,2048]{1,0:T(8,128)(2,1)S(1)} %get-tuple-element.29), channel_id=1, source_target_pairs={{0,8},{8,0},{16,24},{24,16},{32,40},{40,32},{48,56},{56,48},{64,72... | collective-permute-start | bytes 98312 | tf_op jit(solution)/shard_map/ppermute | solution.py:392
  13.1 0.7 %collective-permute-start.1 = (bf16[8,2048]{1,0:T(8,128)(2,1)S(1)}, bf16[8,2048]{1,0:T(8,128)(2,1)S(1)}, u32[]{:S(2)}, u32[]{:S(2)}) collective-permute-start(bf16[8,2048]{1,0:T(8,128)(2,1)S(1)} %get-tuple-element.30), channel_id=1, source_target_pairs={{8,16},{16,8},{24,32},{32,24},{40,48},{48,40},{56,64},{64,56},{72,... | collective-permute-start | bytes 98312 | tf_op jit(solution)/shard_map/ppermute | solution.py:393
  14.4 4.7 %lookup.1 = (f32[3,16,8,2176]{3,2,1,0:T(8,128)S(1)}, f32[16,8,2176]{2,1,0:T(8,128)S(1)}, f32[16,8,2176]{2,1,0:T(8,128)S(1)}, f32[8,2176]{1,0:T(8,128)S(1)}, f32[...) custom-call(s32[1]{0:T(128)S(6)} %copy.5.shear_ref, ...), custom_call_target="tpu_custom_call" | custom-call | flops 30000000 | bytes 10000000 | tf_op jit(solution)/shard_map/lookup/pallas_call | solution.py:396
  19.1 0.0 collective-permute-done.slice_a_ref
  19.2 0.0 collective-permute-done.1.slice_b_ref
  19.2 0.0 collective-permute-done.2.row_a_ref
  19.2 0.0 collective-permute-done.3.row_b_ref
  19.2 2.5 %shade.1 = s16[64,8,128]{2,1,0:T(8,128)(2,1)S(1)} custom-call(s32[1]{0:T(128)S(6)} %copy.5.shear_ref, f32[3,16,8,2176]{3,2,1,0:T(8,128)S(1)} %get-tuple-element.22.sample_ref, f32[16,8,2176]{2,1,0:T(8,128)S(1)} %get-tuple-element.23.front_ref, f32[16,8,2176]{2,1,0:T(8,128)S(1)} %get-tuple-element.24.back_ref, f32[8,2176]{1,0:T(8,128)S(1)} %get-tuple-element.25.alpha_ref, ...), custom_call_target="tpu_custom_call" | custom-call | tf_op jit(solution)/shard_map/shade/pallas_call | solution.py:407
  21.7 28.5 %all_to_all.5.parts_ref = s16[64,8,128]{2,1,0:T(8,128)(2,1)} all-to-all(s16[64,8,128]{2,1,0:T(8,128)(2,1)S(1)} %shade.1), channel_id=1, replica_groups={{288,296,304,312,320,328,336,344,352,360,368,376,384,392,400,408,416,42..., dimensions={0} | all-to-all | bytes 262144 | tf_op jit(solution)/shard_map/all_to_all | solution.py:420
  50.1 1.8 %merge.1 = f32[4,8,32]{2,1,0:T(8,128)} custom-call(s32[1]{0:T(128)S(6)} %copy.5.shear_ref, s16[64,8,128]{2,1,0:T(8,128)(2,1)} %all_to_all.5.parts_ref), custom_call_target="tpu_custom_call" | custom-call | tf_op jit(solution)/shard_map/merge/pallas_call | solution.py:421
Async XLA Ops:
  1.3 17.9 %collective-permute-start.2 = (bf16[16,2048]{1,0:T(8,128)(2,1)S(1)}, bf16[16,2048]{1,0:T(8,128)(2,1)S(1)}, u32[]{:S(2)}, u32[]{:S(2)}) collective-permute-start(bf16[16,2048]{1,0:T(8,128)(2,1)S(1)} %get-tuple-element.31), channel_id=1, source_target_pairs={{0,1},{1,0},{2,3},{3,2},{4,5},{5,4},{6,7},{7,6},{8,9},{9,8},{10,11... | collective-permute-start | bytes 196616 | tf_op jit(solution)/shard_map/ppermute | solution.py:390
  3.2 16.0 %collective-permute-start.3 = (bf16[16,2048]{1,0:T(8,128)(2,1)S(1)}, bf16[16,2048]{1,0:T(8,128)(2,1)S(1)}, u32[]{:S(2)}, u32[]{:S(2)}) collective-permute-start(bf16[16,2048]{1,0:T(8,128)(2,1)S(1)} %get-tuple-element.32), channel_id=1, source_target_pairs={{1,2},{2,1},{3,4},{4,3},{5,6},{6,5},{9,10},{10,9},{11,12},{12,11},... | collective-permute-start | bytes 196616 | tf_op jit(solution)/shard_map/ppermute | solution.py:391
  11.2 8.0 %collective-permute-start = (bf16[8,2048]{1,0:T(8,128)(2,1)S(1)}, bf16[8,2048]{1,0:T(8,128)(2,1)S(1)}, u32[]{:S(2)}, u32[]{:S(2)}) collective-permute-start(bf16[8,2048]{1,0:T(8,128)(2,1)S(1)} %get-tuple-element.29), channel_id=1, source_target_pairs={{0,8},{8,0},{16,24},{24,16},{32,40},{40,32},{48,56},{56,48},{64,72... | collective-permute-start | bytes 98312 | tf_op jit(solution)/shard_map/ppermute | solution.py:392
  13.1 6.1 %collective-permute-start.1 = (bf16[8,2048]{1,0:T(8,128)(2,1)S(1)}, bf16[8,2048]{1,0:T(8,128)(2,1)S(1)}, u32[]{:S(2)}, u32[]{:S(2)}) collective-permute-start(bf16[8,2048]{1,0:T(8,128)(2,1)S(1)} %get-tuple-element.30), channel_id=1, source_target_pairs={{8,16},{16,8},{24,32},{32,24},{40,48},{48,40},{56,64},{64,56},{72,... | collective-permute-start | bytes 98312 | tf_op jit(solution)/shard_map/ppermute | solution.py:393

commit v5 on v4

--- a/solution.py
+++ b/solution.py
@@ -18,7 +18,7 @@
 LOG_STEPS = 65534.0 / (LOG_SPAN - 1.85)
 TINY = 1e-12
 TURN = 36
-CHUNKS = 4
+CHUNKS = 2
 LIMIT = 12 * 1024 * 1024
 
 

time: 52.2 us -> 52.1 us (level)
  no operation moved by 1% of the time
where the time goes in v5:
time: 52.1 us; the launch traced here: 51.9 us
  blocking collectives  28.5 us (55%)
  starting transfers between devices  12.4 us (24%)
  Pallas kernels  10.2 us (20%)
  between operations  0.73 us (1%)
    all_to_all x1, blocking collectives, per_device(): lax.all_to_all(bricks, 'wide', split_axis=0, concat_axis=0, axis_index_gr...  28.5 us
    ppermute x1, starting transfers between devices, per_device(): row_b = lax.ppermute(row_b, 'narrow', pairs(8, 1))  7.92 us
    pallas_call x1, Pallas kernels, per_device(): pl.pallas_call(functools.partial(lookup_kernel, depth_total=depth_total,...  4.73 us
    pallas_call x1, Pallas kernels, per_device(): pl.pallas_call(functools.partial(shade_kernel, depth_total=depth_total, p...  2.49 us
    ppermute x1, starting transfers between devices, per_device(): row_a = lax.ppermute(row_a, 'narrow', pairs(8, 0))  1.92 us
    ppermute x1, starting transfers between devices, per_device(): slice_a = lax.ppermute(slice_a, 'wide', pairs(wide, 0))  1.92 us
    pallas_call x1, Pallas kernels, per_device(): pl.pallas_call(merge_kernel, in_specs=[smem, vmem], out_specs=vmem, out_s...  1.85 us
    pallas_call x1, Pallas kernels, per_device(): pl.pallas_call(functools.partial(prepare_kernel, place=place, across=acro...  1.18 us
  transfers between devices with their start and end apart: 4, of which 0 were waited for; matrix products, arithmetic and copies ran while one was open for 0% of the time, Pallas kernels for 9%

profile of v5, /device:TPU:2, one launch (start us, length us, event | category | flops | bytes accessed | tf_op | source)
XLA Modules:
  0.0 51.9 jit_solution(9026549143701424716)
XLA Ops:
  0.0 1.2 %prepare.1 = (f32[16,8,2688]{2,1,0:T(8,128)S(1)}, bf16[8,2048]{1,0:T(8,128)(2,1)S(1)}, bf16[8,2048]{1,0:T(8,128)(2,1)S(1)}, bf16[16,2048]{1,0:T(8,128)(2,1)S(1)}...) custom-call(bf16[16,8,2048]{2,1,0:T(8,128)(2,1)} %dens_hbm.1, ...), custom_call_target="tpu_custom_call" | custom-call | tf_op jit(solution)/shard_map/prepare/pallas_call | solution.py:376
  1.2 1.9 %collective-permute-start.2 = (bf16[16,2048]{1,0:T(8,128)(2,1)S(1)}, bf16[16,2048]{1,0:T(8,128)(2,1)S(1)}, u32[]{:S(2)}, u32[]{:S(2)}) collective-permute-start(bf16[16,2048]{1,0:T(8,128)(2,1)S(1)} %get-tuple-element.31), channel_id=1, source_target_pairs={{0,1},{1,0},{2,3},{3,2},{4,5},{5,4},{6,7},{7,6},{8,9},{9,8},{10,11... | collective-permute-start | bytes 196616 | tf_op jit(solution)/shard_map/ppermute | solution.py:390
  3.1 7.9 %collective-permute-start.3 = (bf16[16,2048]{1,0:T(8,128)(2,1)S(1)}, bf16[16,2048]{1,0:T(8,128)(2,1)S(1)}, u32[]{:S(2)}, u32[]{:S(2)}) collective-permute-start(bf16[16,2048]{1,0:T(8,128)(2,1)S(1)} %get-tuple-element.32), channel_id=1, source_target_pairs={{1,2},{2,1},{3,4},{4,3},{5,6},{6,5},{9,10},{10,9},{11,12},{12,11},... | collective-permute-start | bytes 196616 | tf_op jit(solution)/shard_map/ppermute | solution.py:391
  11.0 1.9 %collective-permute-start = (bf16[8,2048]{1,0:T(8,128)(2,1)S(1)}, bf16[8,2048]{1,0:T(8,128)(2,1)S(1)}, u32[]{:S(2)}, u32[]{:S(2)}) collective-permute-start(bf16[8,2048]{1,0:T(8,128)(2,1)S(1)} %get-tuple-element.29), channel_id=1, source_target_pairs={{0,8},{8,0},{16,24},{24,16},{32,40},{40,32},{48,56},{56,48},{64,72... | collective-permute-start | bytes 98312 | tf_op jit(solution)/shard_map/ppermute | solution.py:392
  13.0 0.7 %collective-permute-start.1 = (bf16[8,2048]{1,0:T(8,128)(2,1)S(1)}, bf16[8,2048]{1,0:T(8,128)(2,1)S(1)}, u32[]{:S(2)}, u32[]{:S(2)}) collective-permute-start(bf16[8,2048]{1,0:T(8,128)(2,1)S(1)} %get-tuple-element.30), channel_id=1, source_target_pairs={{8,16},{16,8},{24,32},{32,24},{40,48},{48,40},{56,64},{64,56},{72,... | collective-permute-start | bytes 98312 | tf_op jit(solution)/shard_map/ppermute | solution.py:393
  14.3 4.7 %lookup.1 = (f32[3,16,8,2176]{3,2,1,0:T(8,128)S(1)}, f32[16,8,2176]{2,1,0:T(8,128)S(1)}, f32[16,8,2176]{2,1,0:T(8,128)S(1)}, f32[8,2176]{1,0:T(8,128)S(1)}, f32[...) custom-call(s32[1]{0:T(128)S(6)} %copy.5.shear_ref, ...), custom_call_target="tpu_custom_call" | custom-call | flops 30000000 | bytes 10000000 | tf_op jit(solution)/shard_map/lookup/pallas_call | solution.py:396
  19.0 0.0 collective-permute-done.slice_a_ref
  19.0 0.0 collective-permute-done.1.slice_b_ref
  19.0 0.0 collective-permute-done.2.row_a_ref
  19.1 0.0 collective-permute-done.3.row_b_ref
  19.1 2.5 %shade.1 = s16[64,8,128]{2,1,0:T(8,128)(2,1)S(1)} custom-call(s32[1]{0:T(128)S(6)} %copy.5.shear_ref, f32[3,16,8,2176]{3,2,1,0:T(8,128)S(1)} %get-tuple-element.22.sample_ref, f32[16,8,2176]{2,1,0:T(8,128)S(1)} %get-tuple-element.23.front_ref, f32[16,8,2176]{2,1,0:T(8,128)S(1)} %get-tuple-element.24.back_ref, f32[8,2176]{1,0:T(8,128)S(1)} %get-tuple-element.25.alpha_ref, ...), custom_call_target="tpu_custom_call" | custom-call | tf_op jit(solution)/shard_map/shade/pallas_call | solution.py:407
  21.6 28.5 %all_to_all.5.parts_ref = s16[64,8,128]{2,1,0:T(8,128)(2,1)} all-to-all(s16[64,8,128]{2,1,0:T(8,128)(2,1)S(1)} %shade.1), channel_id=1, replica_groups={{288,296,304,312,320,328,336,344,352,360,368,376,384,392,400,408,416,42..., dimensions={0} | all-to-all | bytes 262144 | tf_op jit(solution)/shard_map/all_to_all | solution.py:420
  50.0 1.8 %merge.1 = f32[4,8,32]{2,1,0:T(8,128)} custom-call(s32[1]{0:T(128)S(6)} %copy.5.shear_ref, s16[64,8,128]{2,1,0:T(8,128)(2,1)} %all_to_all.5.parts_ref), custom_call_target="tpu_custom_call" | custom-call | tf_op jit(solution)/shard_map/merge/pallas_call | solution.py:421
Async XLA Ops:
  1.2 17.9 %collective-permute-start.2 = (bf16[16,2048]{1,0:T(8,128)(2,1)S(1)}, bf16[16,2048]{1,0:T(8,128)(2,1)S(1)}, u32[]{:S(2)}, u32[]{:S(2)}) collective-permute-start(bf16[16,2048]{1,0:T(8,128)(2,1)S(1)} %get-tuple-element.31), channel_id=1, source_target_pairs={{0,1},{1,0},{2,3},{3,2},{4,5},{5,4},{6,7},{7,6},{8,9},{9,8},{10,11... | collective-permute-start | bytes 196616 | tf_op jit(solution)/shard_map/ppermute | solution.py:390
  3.1 15.9 %collective-permute-start.3 = (bf16[16,2048]{1,0:T(8,128)(2,1)S(1)}, bf16[16,2048]{1,0:T(8,128)(2,1)S(1)}, u32[]{:S(2)}, u32[]{:S(2)}) collective-permute-start(bf16[16,2048]{1,0:T(8,128)(2,1)S(1)} %get-tuple-element.32), channel_id=1, source_target_pairs={{1,2},{2,1},{3,4},{4,3},{5,6},{6,5},{9,10},{10,9},{11,12},{12,11},... | collective-permute-start | bytes 196616 | tf_op jit(solution)/shard_map/ppermute | solution.py:391
  11.0 8.0 %collective-permute-start = (bf16[8,2048]{1,0:T(8,128)(2,1)S(1)}, bf16[8,2048]{1,0:T(8,128)(2,1)S(1)}, u32[]{:S(2)}, u32[]{:S(2)}) collective-permute-start(bf16[8,2048]{1,0:T(8,128)(2,1)S(1)} %get-tuple-element.29), channel_id=1, source_target_pairs={{0,8},{8,0},{16,24},{24,16},{32,40},{40,32},{48,56},{56,48},{64,72... | collective-permute-start | bytes 98312 | tf_op jit(solution)/shard_map/ppermute | solution.py:392
  13.0 6.1 %collective-permute-start.1 = (bf16[8,2048]{1,0:T(8,128)(2,1)S(1)}, bf16[8,2048]{1,0:T(8,128)(2,1)S(1)}, u32[]{:S(2)}, u32[]{:S(2)}) collective-permute-start(bf16[8,2048]{1,0:T(8,128)(2,1)S(1)} %get-tuple-element.30), channel_id=1, source_target_pairs={{8,16},{16,8},{24,32},{32,24},{40,48},{48,40},{56,64},{64,56},{72,... | collective-permute-start | bytes 98312 | tf_op jit(solution)/shard_map/ppermute | solution.py:393
